TPU v7x, 128 devices: a whole 4x4x4 slice. The times are simulated.
128 devices in a mesh: ctx: 16 (over z_lo, y, core), head: 8 (over z_hi, x).
Axes of the slice: x: 4, y: 4, z: 4 (z_hi: 2, z_lo: 2; z = z_hi * 2 + z_lo), core: 2. Of those that a mesh axis runs over, the one named last changes fastest.
Arguments:
- tokens: bfloat16 [8192, 8192], P('ctx'), may hold values from -210 to 210
- positions: int32 [8192], P('ctx'), may hold values from 0 to 8191, each once
- stored_qkv: bfloat16 [8192, 6144], P(('ctx', 'head')), may hold values from -0.109375 to 0.109375
- block_order: int32 [64], replicated, may hold values from 0 to 63, each once
- qkv_bias: float32 [6144], P('head'), may hold values from -3 to 3
Outputs:
- attended: bfloat16 [8192, 4096], P('ctx', 'head')
Inputs may be any that keep to these rules, and one draw needn't show every extreme that they name: `positions`: each position of 0 to 8191 appears once. `block_order`: each row block appears once.
All inputs are finite; a program needn't handle non-finite values.
Results may differ from a plain program's by a relative error of at most 0.04.
Values may be sent and summed in bfloat16 or wider, within the bound.
No kernel may reach another device: no remote copies, remote signals or barrier semaphores. Data moves between devices by JAX's collectives and lax.ppermute only.
A program may use at most 128 MiB of HBM per device.

v0:
```python
import math

import jax
import jax.numpy as jnp
from jax import lax
from jax.sharding import PartitionSpec as P

HEAD_DIM = 128
QPG = 4


theta_base = 1000000.0


def from_behind(block, axis, distance):
    devices = range(lax.axis_size(axis))
    route = [((i - distance) % len(devices), i) for i in devices]
    return lax.ppermute(block, axis, route)


def angles(positions, width):
    half = width // 2
    freq = jnp.exp(jnp.arange(half, dtype=jnp.float32) * (-2.0 * math.log(theta_base) / width))
    phase = positions.astype(jnp.float32)[:, None] * freq[None, :]
    return (jnp.cos(phase), jnp.sin(phase))


def rotate(values, cosine, sine):
    half = values.shape[-1] // 2
    first = values[..., :half]
    second = values[..., half:]
    return jnp.concatenate(
        [first * cosine - second * sine, second * cosine + first * sine], axis=-1
    )


def local(tokens, positions, stored_qkv, block_order, qkv_bias):
    rows_dev, width = tokens.shape
    blocks = block_order.shape[0]
    ordered = tokens.reshape(rows_dev, blocks, width // blocks)[:, block_order, :].reshape(
        rows_dev, width
    )
    mine = lax.all_to_all(stored_qkv, "head", split_axis=1, concat_axis=0, tiled=True)
    weight = lax.all_gather(mine, "ctx", axis=0, tiled=True)
    qkv = jnp.dot(ordered, weight, preferred_element_type=jnp.float32)
    qkv = qkv + qkv_bias[None, :]
    groups = qkv.shape[1] // ((QPG + 2) * HEAD_DIM)
    qkv = qkv.reshape(rows_dev, groups, QPG + 2, HEAD_DIM)
    cosine, sine = angles(positions, HEAD_DIM)
    turned = rotate(qkv[:, :, : QPG + 1], cosine[:, None, None, :], sine[:, None, None, :])
    queries = turned[:, :, :QPG].astype(jnp.bfloat16)
    pairs = jnp.concatenate([turned[:, :, QPG], qkv[:, :, QPG + 1]], axis=-1).astype(jnp.bfloat16)
    scale = 1.0 / math.sqrt(HEAD_DIM)

    def absorb(state, block):
        best, total, accum = state
        keyvals, key_pos = block
        keys = keyvals[..., :HEAD_DIM]
        values = keyvals[..., HEAD_DIM:]
        score = (
            jnp.einsum("rghd,kgd->ghrk", queries, keys, preferred_element_type=jnp.float32) * scale
        )
        allowed = (key_pos[None, :] <= positions[:, None])[None, None]
        score = jnp.where(allowed, score, -1e30)
        newest = jnp.maximum(best, jnp.max(score, axis=-1))
        prob = jnp.where(allowed, jnp.exp(score - newest[..., None]), 0.0)
        factor = jnp.exp(best - newest)
        total = total * factor + jnp.sum(prob, axis=-1)
        accum = accum * factor[..., None] + jnp.einsum(
            "ghrk,kgd->ghrd", prob.astype(jnp.bfloat16), values, preferred_element_type=jnp.float32
        )
        return (newest, total, accum)

    start_state = (
        jnp.full((groups, QPG, rows_dev), -1e30, jnp.float32),
        jnp.zeros((groups, QPG, rows_dev), jnp.float32),
        jnp.zeros((groups, QPG, rows_dev, HEAD_DIM), jnp.float32),
    )
    own_block = (pairs, positions)
    cycle_size = lax.axis_size("ctx")
    state = absorb(start_state, own_block)

    def turn(step, carry):
        current, block = carry
        block = from_behind((block[0], block[1]), "ctx", 1)
        return (absorb(current, block), block)

    state, last_block = lax.fori_loop(0, cycle_size - 1, turn, (state, own_block))
    best, total, accum = state
    result = accum / total[..., None]
    return (
        jnp.transpose(result, (2, 0, 1, 3))
        .reshape(rows_dev, groups * QPG * HEAD_DIM)
        .astype(jnp.bfloat16)
    )


def solution(mesh):
    placed = (P("ctx", None), P("ctx"), P(("ctx", "head"), None), P(), P("head"))
    return jax.shard_map(
        local, mesh=mesh, in_specs=placed, out_specs=P("ctx", "head"), check_vma=False
    )
```

profile of v0, /device:TPU:0, one launch (start us, length us, event | category | flops | bytes accessed | tf_op | source)
XLA Modules:
  0.0 321.7 jit_solution(8581330215154033254)
XLA Ops:
  7.7 22.0 %all_to_all.19 = bf16[64,8,768]{2,0,1:T(8,128)(2,1)} all-to-all(bf16[64,8,768]{2,0,1:T(8,128)(2,1)S(1)} %bitcast.159), channel_id=1, replica_groups=mesh['ctx'=16,'head'=8] {'head'}, dimensions={1} | all-to-all | bytes 1572864 | tf_op jit(solution)/shard_map/all_to_all | solution.py:43
  31.1 12.0 %copy.31 = bf16[512,8192]{0,1:T(8,128)(2,1)} copy(bf16[512,8192]{1,0:T(8,128)(2,1)} %param.7) | data formatting | bytes 16777216 | tf_op args[0]
  43.1 11.2 %copy.32 = bf16[512,64,128]{2,0,1:T(8,128)(2,1)} copy(bf16[512,64,128]{0,2,1:T(8,128)(2,1)} %bitcast.152) | data formatting | bytes 16777216 | tf_op jit(solution)/shard_map/reshape | solution.py:40
  54.3 9.2 %gather_fusion = bf16[64,512,128]{2,1,0:T(8,128)(2,1)} fusion(bf16[512,64,128]{2,0,1:T(8,128)(2,1)} %copy.32, s32[1024]{0:T(1024)S(1)} %pad_clamp_fusion), kind=kCustom, calls=%fused_computation | custom fusion | bytes 16777472 | tf_op jit(solution)/shard_map/gather | solution.py:40
  63.5 12.0 %copy.33 = bf16[512,64,128]{0,2,1:T(8,128)(2,1)} copy(bf16[512,64,128]{2,0,1:T(8,128)(2,1)} %bitcast.151) | data formatting | bytes 16777216 | tf_op jit(solution)/shard_map/gather | solution.py:40
  77.4 21.9 %all-gather.2.cloned.1.call-done = bf16[8192,768]{1,0:T(8,128)(2,1)} async-done(((bf16[512,768]{1,0:T(8,128)(2,1)}), bf16[8192,768]{1,0:T(8,128)(2,1)}) %all-gather.2.cloned.1.call-update) | async-done | bytes 12582928 | tf_op jit(solution)/shard_map/all_gather | solution.py:44
  99.4 13.6 %convolution_add_fusion = f32[512,768]{1,0:T(8,128)} fusion(bf16[512,8192]{0,1:T(8,128)(2,1)} %bitcast.153, bf16[8192,768]{1,0:T(8,128)(2,1)} %all-gather.2.cloned.1.call-done, f32[768]{0:T(1024)S(1)} %copy-done.4), kind=kOutput, calls=%fused_computation.31 | convolution fusion | flops 6442844160 | bytes 22547456 | tf_op jit(solution)/shard_map/dot_general | solution.py:45
  117.6 2.6 copy.44
  122.3 2.8 fusion.19
  125.3 3.4 %fusion.21 = f32[4,512]{1,0:T(4,128)S(1)} fusion(f32[512,512,4]{1,0,2:T(8,128)} %get-tuple-element.80, f32[4,512]{1,0:T(4,128)S(1)} %get-tuple-element.76, pred[512,512]{0,1:T(8,128)(4,1)S(1)} %copy-done.2), kind=kLoop, calls=%fused_computation.27 | loop fusion | flops 5240832 | bytes 4472832 | tf_op jit(solution)/shard_map/reduce_sum | solution.py:68
  130.4 182.8 %while.18 = (s32[]{:T(128)}, f32[1,4,512]{2,1,0:T(4,128)S(1)}, f32[1,4,512]{2,1,0:T(4,128)S(1)}, f32[1,4,512,128]{3,2,1,0:T(8,128)S(1)}, bf16[512,1,256]{2,0,1:T...) while((s32[]{:T(128)}, f32[1,4,512]{2,1,0:T(4,128)S(1)}, ...), condition=%wide.region_5.6_spmd, body=%wide.region_2.5_spmd.sunk | while | flops 551294976 | bytes 18235564 | solution.py:88
  132.1 6.5 %collective-permute-done = s32[512]{0:T(512)S(1)} collective-permute-done((s32[512]{0:T(512)S(1)}, s32[512]{0:T(512)S(1)}, u32[]{:S(2)}, u32[]{:S(2)}) %collective-permute-start) | collective-permute-done | bytes 2080 | tf_op jit(solution)/shard_map/while/body/eval_jaxpr/ppermute | solution.py:18
  140.8 1.9 fusion.55
  142.9 7.8 %collective-permute-done = s32[512]{0:T(512)S(1)} collective-permute-done((s32[512]{0:T(512)S(1)}, s32[512]{0:T(512)S(1)}, u32[]{:S(2)}, u32[]{:S(2)}) %collective-permute-start) | collective-permute-done | bytes 2080 | tf_op jit(solution)/shard_map/while/body/eval_jaxpr/ppermute | solution.py:18
  155.1 7.8 %collective-permute-done = s32[512]{0:T(512)S(1)} collective-permute-done((s32[512]{0:T(512)S(1)}, s32[512]{0:T(512)S(1)}, u32[]{:S(2)}, u32[]{:S(2)}) %collective-permute-start) | collective-permute-done | bytes 2080 | tf_op jit(solution)/shard_map/while/body/eval_jaxpr/ppermute | solution.py:18
  165.2 1.9 fusion.55
  167.3 7.8 %collective-permute-done = s32[512]{0:T(512)S(1)} collective-permute-done((s32[512]{0:T(512)S(1)}, s32[512]{0:T(512)S(1)}, u32[]{:S(2)}, u32[]{:S(2)}) %collective-permute-start) | collective-permute-done | bytes 2080 | tf_op jit(solution)/shard_map/while/body/eval_jaxpr/ppermute | solution.py:18
  179.5 7.8 %collective-permute-done = s32[512]{0:T(512)S(1)} collective-permute-done((s32[512]{0:T(512)S(1)}, s32[512]{0:T(512)S(1)}, u32[]{:S(2)}, u32[]{:S(2)}) %collective-permute-start) | collective-permute-done | bytes 2080 | tf_op jit(solution)/shard_map/while/body/eval_jaxpr/ppermute | solution.py:18
  189.5 1.9 fusion.55
  191.6 7.8 %collective-permute-done = s32[512]{0:T(512)S(1)} collective-permute-done((s32[512]{0:T(512)S(1)}, s32[512]{0:T(512)S(1)}, u32[]{:S(2)}, u32[]{:S(2)}) %collective-permute-start) | collective-permute-done | bytes 2080 | tf_op jit(solution)/shard_map/while/body/eval_jaxpr/ppermute | solution.py:18
  203.8 7.8 %collective-permute-done = s32[512]{0:T(512)S(1)} collective-permute-done((s32[512]{0:T(512)S(1)}, s32[512]{0:T(512)S(1)}, u32[]{:S(2)}, u32[]{:S(2)}) %collective-permute-start) | collective-permute-done | bytes 2080 | tf_op jit(solution)/shard_map/while/body/eval_jaxpr/ppermute | solution.py:18
  213.9 1.9 fusion.55
  216.0 7.8 %collective-permute-done = s32[512]{0:T(512)S(1)} collective-permute-done((s32[512]{0:T(512)S(1)}, s32[512]{0:T(512)S(1)}, u32[]{:S(2)}, u32[]{:S(2)}) %collective-permute-start) | collective-permute-done | bytes 2080 | tf_op jit(solution)/shard_map/while/body/eval_jaxpr/ppermute | solution.py:18
  228.1 7.8 %collective-permute-done = s32[512]{0:T(512)S(1)} collective-permute-done((s32[512]{0:T(512)S(1)}, s32[512]{0:T(512)S(1)}, u32[]{:S(2)}, u32[]{:S(2)}) %collective-permute-start) | collective-permute-done | bytes 2080 | tf_op jit(solution)/shard_map/while/body/eval_jaxpr/ppermute | solution.py:18
  238.2 1.9 fusion.55
  240.3 7.8 %collective-permute-done = s32[512]{0:T(512)S(1)} collective-permute-done((s32[512]{0:T(512)S(1)}, s32[512]{0:T(512)S(1)}, u32[]{:S(2)}, u32[]{:S(2)}) %collective-permute-start) | collective-permute-done | bytes 2080 | tf_op jit(solution)/shard_map/while/body/eval_jaxpr/ppermute | solution.py:18
  252.5 7.8 %collective-permute-done = s32[512]{0:T(512)S(1)} collective-permute-done((s32[512]{0:T(512)S(1)}, s32[512]{0:T(512)S(1)}, u32[]{:S(2)}, u32[]{:S(2)}) %collective-permute-start) | collective-permute-done | bytes 2080 | tf_op jit(solution)/shard_map/while/body/eval_jaxpr/ppermute | solution.py:18
  262.6 1.9 fusion.55
  264.7 7.8 %collective-permute-done = s32[512]{0:T(512)S(1)} collective-permute-done((s32[512]{0:T(512)S(1)}, s32[512]{0:T(512)S(1)}, u32[]{:S(2)}, u32[]{:S(2)}) %collective-permute-start) | collective-permute-done | bytes 2080 | tf_op jit(solution)/shard_map/while/body/eval_jaxpr/ppermute | solution.py:18
  276.8 7.8 %collective-permute-done = s32[512]{0:T(512)S(1)} collective-permute-done((s32[512]{0:T(512)S(1)}, s32[512]{0:T(512)S(1)}, u32[]{:S(2)}, u32[]{:S(2)}) %collective-permute-start) | collective-permute-done | bytes 2080 | tf_op jit(solution)/shard_map/while/body/eval_jaxpr/ppermute | solution.py:18
  289.0 7.8 %collective-permute-done = s32[512]{0:T(512)S(1)} collective-permute-done((s32[512]{0:T(512)S(1)}, s32[512]{0:T(512)S(1)}, u32[]{:S(2)}, u32[]{:S(2)}) %collective-permute-start) | collective-permute-done | bytes 2080 | tf_op jit(solution)/shard_map/while/body/eval_jaxpr/ppermute | solution.py:18
  301.2 7.8 %collective-permute-done = s32[512]{0:T(512)S(1)} collective-permute-done((s32[512]{0:T(512)S(1)}, s32[512]{0:T(512)S(1)}, u32[]{:S(2)}, u32[]{:S(2)}) %collective-permute-start) | collective-permute-done | bytes 2080 | tf_op jit(solution)/shard_map/while/body/eval_jaxpr/ppermute | solution.py:18
  (211 shorter events, 68.3 us)
Async XLA Ops:
  6.5 92.8 %all-gather.2.cloned.1.call-start = ((), (), s32[]{:S(2)}) async-start(), calls=%async_computation.1 | async-start | bytes 13369344 | tf_op jit(solution)/shard_map/all_gather | solution.py:44
  63.5 35.8 %copy-start.4 = (f32[768]{0:T(1024)S(1)}, f32[768]{0:T(1024)}, u32[]{:S(2)}) copy-start(f32[768]{0:T(1024)} %param.11) | copy-start | bytes 9220
  130.6 8.2 %collective-permute-start.1 = (bf16[512,1,256]{2,0,1:T(8,128)(2,1)S(1)}, bf16[512,1,256]{2,0,1:T(8,128)(2,1)S(1)}, u32[]{:S(2)}, u32[]{:S(2)}) collective-permute-start(bf16[512,1,256]{2,0,1:T(8,128)(2,1)S(1)} %get-tuple-element.151), channel_id=1, source_target_pairs={{120,0},{0,8},{8,16},{16,24},{24,32},{32,40},{40,48},{48,56},{56,6... | collective-permute-start | bytes 786440 | tf_op jit(solution)/shard_map/while/body/eval_jaxpr/ppermute | solution.py:18
  130.9 7.7 %collective-permute-start = (s32[512]{0:T(512)S(1)}, s32[512]{0:T(512)S(1)}, u32[]{:S(2)}, u32[]{:S(2)}) collective-permute-start(s32[512]{0:T(512)S(1)} %get-tuple-element.152), channel_id=1, source_target_pairs={{120,0},{0,8},{8,16},{16,24},{24,32},{32,40},{40,48},{48,56},{56,6... | collective-permute-start | bytes 6152 | tf_op jit(solution)/shard_map/while/body/eval_jaxpr/ppermute | solution.py:18
  142.8 8.2 %collective-permute-start.1 = (bf16[512,1,256]{2,0,1:T(8,128)(2,1)S(1)}, bf16[512,1,256]{2,0,1:T(8,128)(2,1)S(1)}, u32[]{:S(2)}, u32[]{:S(2)}) collective-permute-start(bf16[512,1,256]{2,0,1:T(8,128)(2,1)S(1)} %get-tuple-element.151), channel_id=1, source_target_pairs={{120,0},{0,8},{8,16},{16,24},{24,32},{32,40},{40,48},{48,56},{56,6... | collective-permute-start | bytes 786440 | tf_op jit(solution)/shard_map/while/body/eval_jaxpr/ppermute | solution.py:18
  142.9 7.9 %collective-permute-start = (s32[512]{0:T(512)S(1)}, s32[512]{0:T(512)S(1)}, u32[]{:S(2)}, u32[]{:S(2)}) collective-permute-start(s32[512]{0:T(512)S(1)} %get-tuple-element.152), channel_id=1, source_target_pairs={{120,0},{0,8},{8,16},{16,24},{24,32},{32,40},{40,48},{48,56},{56,6... | collective-permute-start | bytes 6152 | tf_op jit(solution)/shard_map/while/body/eval_jaxpr/ppermute | solution.py:18
  154.9 8.2 %collective-permute-start.1 = (bf16[512,1,256]{2,0,1:T(8,128)(2,1)S(1)}, bf16[512,1,256]{2,0,1:T(8,128)(2,1)S(1)}, u32[]{:S(2)}, u32[]{:S(2)}) collective-permute-start(bf16[512,1,256]{2,0,1:T(8,128)(2,1)S(1)} %get-tuple-element.151), channel_id=1, source_target_pairs={{120,0},{0,8},{8,16},{16,24},{24,32},{32,40},{40,48},{48,56},{56,6... | collective-permute-start | bytes 786440 | tf_op jit(solution)/shard_map/while/body/eval_jaxpr/ppermute | solution.py:18
  155.0 7.9 %collective-permute-start = (s32[512]{0:T(512)S(1)}, s32[512]{0:T(512)S(1)}, u32[]{:S(2)}, u32[]{:S(2)}) collective-permute-start(s32[512]{0:T(512)S(1)} %get-tuple-element.152), channel_id=1, source_target_pairs={{120,0},{0,8},{8,16},{16,24},{24,32},{32,40},{40,48},{48,56},{56,6... | collective-permute-start | bytes 6152 | tf_op jit(solution)/shard_map/while/body/eval_jaxpr/ppermute | solution.py:18
  167.1 8.2 %collective-permute-start.1 = (bf16[512,1,256]{2,0,1:T(8,128)(2,1)S(1)}, bf16[512,1,256]{2,0,1:T(8,128)(2,1)S(1)}, u32[]{:S(2)}, u32[]{:S(2)}) collective-permute-start(bf16[512,1,256]{2,0,1:T(8,128)(2,1)S(1)} %get-tuple-element.151), channel_id=1, source_target_pairs={{120,0},{0,8},{8,16},{16,24},{24,32},{32,40},{40,48},{48,56},{56,6... | collective-permute-start | bytes 786440 | tf_op jit(solution)/shard_map/while/body/eval_jaxpr/ppermute | solution.py:18
  167.2 7.9 %collective-permute-start = (s32[512]{0:T(512)S(1)}, s32[512]{0:T(512)S(1)}, u32[]{:S(2)}, u32[]{:S(2)}) collective-permute-start(s32[512]{0:T(512)S(1)} %get-tuple-element.152), channel_id=1, source_target_pairs={{120,0},{0,8},{8,16},{16,24},{24,32},{32,40},{40,48},{48,56},{56,6... | collective-permute-start | bytes 6152 | tf_op jit(solution)/shard_map/while/body/eval_jaxpr/ppermute | solution.py:18
  179.3 8.2 %collective-permute-start.1 = (bf16[512,1,256]{2,0,1:T(8,128)(2,1)S(1)}, bf16[512,1,256]{2,0,1:T(8,128)(2,1)S(1)}, u32[]{:S(2)}, u32[]{:S(2)}) collective-permute-start(bf16[512,1,256]{2,0,1:T(8,128)(2,1)S(1)} %get-tuple-element.151), channel_id=1, source_target_pairs={{120,0},{0,8},{8,16},{16,24},{24,32},{32,40},{40,48},{48,56},{56,6... | collective-permute-start | bytes 786440 | tf_op jit(solution)/shard_map/while/body/eval_jaxpr/ppermute | solution.py:18
  179.4 7.9 %collective-permute-start = (s32[512]{0:T(512)S(1)}, s32[512]{0:T(512)S(1)}, u32[]{:S(2)}, u32[]{:S(2)}) collective-permute-start(s32[512]{0:T(512)S(1)} %get-tuple-element.152), channel_id=1, source_target_pairs={{120,0},{0,8},{8,16},{16,24},{24,32},{32,40},{40,48},{48,56},{56,6... | collective-permute-start | bytes 6152 | tf_op jit(solution)/shard_map/while/body/eval_jaxpr/ppermute | solution.py:18
  191.5 8.2 %collective-permute-start.1 = (bf16[512,1,256]{2,0,1:T(8,128)(2,1)S(1)}, bf16[512,1,256]{2,0,1:T(8,128)(2,1)S(1)}, u32[]{:S(2)}, u32[]{:S(2)}) collective-permute-start(bf16[512,1,256]{2,0,1:T(8,128)(2,1)S(1)} %get-tuple-element.151), channel_id=1, source_target_pairs={{120,0},{0,8},{8,16},{16,24},{24,32},{32,40},{40,48},{48,56},{56,6... | collective-permute-start | bytes 786440 | tf_op jit(solution)/shard_map/while/body/eval_jaxpr/ppermute | solution.py:18
  191.5 7.9 %collective-permute-start = (s32[512]{0:T(512)S(1)}, s32[512]{0:T(512)S(1)}, u32[]{:S(2)}, u32[]{:S(2)}) collective-permute-start(s32[512]{0:T(512)S(1)} %get-tuple-element.152), channel_id=1, source_target_pairs={{120,0},{0,8},{8,16},{16,24},{24,32},{32,40},{40,48},{48,56},{56,6... | collective-permute-start | bytes 6152 | tf_op jit(solution)/shard_map/while/body/eval_jaxpr/ppermute | solution.py:18
  203.6 8.2 %collective-permute-start.1 = (bf16[512,1,256]{2,0,1:T(8,128)(2,1)S(1)}, bf16[512,1,256]{2,0,1:T(8,128)(2,1)S(1)}, u32[]{:S(2)}, u32[]{:S(2)}) collective-permute-start(bf16[512,1,256]{2,0,1:T(8,128)(2,1)S(1)} %get-tuple-element.151), channel_id=1, source_target_pairs={{120,0},{0,8},{8,16},{16,24},{24,32},{32,40},{40,48},{48,56},{56,6... | collective-permute-start | bytes 786440 | tf_op jit(solution)/shard_map/while/body/eval_jaxpr/ppermute | solution.py:18
  203.7 7.9 %collective-permute-start = (s32[512]{0:T(512)S(1)}, s32[512]{0:T(512)S(1)}, u32[]{:S(2)}, u32[]{:S(2)}) collective-permute-start(s32[512]{0:T(512)S(1)} %get-tuple-element.152), channel_id=1, source_target_pairs={{120,0},{0,8},{8,16},{16,24},{24,32},{32,40},{40,48},{48,56},{56,6... | collective-permute-start | bytes 6152 | tf_op jit(solution)/shard_map/while/body/eval_jaxpr/ppermute | solution.py:18
  215.8 8.2 %collective-permute-start.1 = (bf16[512,1,256]{2,0,1:T(8,128)(2,1)S(1)}, bf16[512,1,256]{2,0,1:T(8,128)(2,1)S(1)}, u32[]{:S(2)}, u32[]{:S(2)}) collective-permute-start(bf16[512,1,256]{2,0,1:T(8,128)(2,1)S(1)} %get-tuple-element.151), channel_id=1, source_target_pairs={{120,0},{0,8},{8,16},{16,24},{24,32},{32,40},{40,48},{48,56},{56,6... | collective-permute-start | bytes 786440 | tf_op jit(solution)/shard_map/while/body/eval_jaxpr/ppermute | solution.py:18
  215.9 7.9 %collective-permute-start = (s32[512]{0:T(512)S(1)}, s32[512]{0:T(512)S(1)}, u32[]{:S(2)}, u32[]{:S(2)}) collective-permute-start(s32[512]{0:T(512)S(1)} %get-tuple-element.152), channel_id=1, source_target_pairs={{120,0},{0,8},{8,16},{16,24},{24,32},{32,40},{40,48},{48,56},{56,6... | collective-permute-start | bytes 6152 | tf_op jit(solution)/shard_map/while/body/eval_jaxpr/ppermute | solution.py:18
  228.0 8.2 %collective-permute-start.1 = (bf16[512,1,256]{2,0,1:T(8,128)(2,1)S(1)}, bf16[512,1,256]{2,0,1:T(8,128)(2,1)S(1)}, u32[]{:S(2)}, u32[]{:S(2)}) collective-permute-start(bf16[512,1,256]{2,0,1:T(8,128)(2,1)S(1)} %get-tuple-element.151), channel_id=1, source_target_pairs={{120,0},{0,8},{8,16},{16,24},{24,32},{32,40},{40,48},{48,56},{56,6... | collective-permute-start | bytes 786440 | tf_op jit(solution)/shard_map/while/body/eval_jaxpr/ppermute | solution.py:18
  228.1 7.9 %collective-permute-start = (s32[512]{0:T(512)S(1)}, s32[512]{0:T(512)S(1)}, u32[]{:S(2)}, u32[]{:S(2)}) collective-permute-start(s32[512]{0:T(512)S(1)} %get-tuple-element.152), channel_id=1, source_target_pairs={{120,0},{0,8},{8,16},{16,24},{24,32},{32,40},{40,48},{48,56},{56,6... | collective-permute-start | bytes 6152 | tf_op jit(solution)/shard_map/while/body/eval_jaxpr/ppermute | solution.py:18
  240.2 8.2 %collective-permute-start.1 = (bf16[512,1,256]{2,0,1:T(8,128)(2,1)S(1)}, bf16[512,1,256]{2,0,1:T(8,128)(2,1)S(1)}, u32[]{:S(2)}, u32[]{:S(2)}) collective-permute-start(bf16[512,1,256]{2,0,1:T(8,128)(2,1)S(1)} %get-tuple-element.151), channel_id=1, source_target_pairs={{120,0},{0,8},{8,16},{16,24},{24,32},{32,40},{40,48},{48,56},{56,6... | collective-permute-start | bytes 786440 | tf_op jit(solution)/shard_map/while/body/eval_jaxpr/ppermute | solution.py:18
  240.2 7.9 %collective-permute-start = (s32[512]{0:T(512)S(1)}, s32[512]{0:T(512)S(1)}, u32[]{:S(2)}, u32[]{:S(2)}) collective-permute-start(s32[512]{0:T(512)S(1)} %get-tuple-element.152), channel_id=1, source_target_pairs={{120,0},{0,8},{8,16},{16,24},{24,32},{32,40},{40,48},{48,56},{56,6... | collective-permute-start | bytes 6152 | tf_op jit(solution)/shard_map/while/body/eval_jaxpr/ppermute | solution.py:18
  252.3 8.2 %collective-permute-start.1 = (bf16[512,1,256]{2,0,1:T(8,128)(2,1)S(1)}, bf16[512,1,256]{2,0,1:T(8,128)(2,1)S(1)}, u32[]{:S(2)}, u32[]{:S(2)}) collective-permute-start(bf16[512,1,256]{2,0,1:T(8,128)(2,1)S(1)} %get-tuple-element.151), channel_id=1, source_target_pairs={{120,0},{0,8},{8,16},{16,24},{24,32},{32,40},{40,48},{48,56},{56,6... | collective-permute-start | bytes 786440 | tf_op jit(solution)/shard_map/while/body/eval_jaxpr/ppermute | solution.py:18
  252.4 7.9 %collective-permute-start = (s32[512]{0:T(512)S(1)}, s32[512]{0:T(512)S(1)}, u32[]{:S(2)}, u32[]{:S(2)}) collective-permute-start(s32[512]{0:T(512)S(1)} %get-tuple-element.152), channel_id=1, source_target_pairs={{120,0},{0,8},{8,16},{16,24},{24,32},{32,40},{40,48},{48,56},{56,6... | collective-permute-start | bytes 6152 | tf_op jit(solution)/shard_map/while/body/eval_jaxpr/ppermute | solution.py:18
  264.5 8.2 %collective-permute-start.1 = (bf16[512,1,256]{2,0,1:T(8,128)(2,1)S(1)}, bf16[512,1,256]{2,0,1:T(8,128)(2,1)S(1)}, u32[]{:S(2)}, u32[]{:S(2)}) collective-permute-start(bf16[512,1,256]{2,0,1:T(8,128)(2,1)S(1)} %get-tuple-element.151), channel_id=1, source_target_pairs={{120,0},{0,8},{8,16},{16,24},{24,32},{32,40},{40,48},{48,56},{56,6... | collective-permute-start | bytes 786440 | tf_op jit(solution)/shard_map/while/body/eval_jaxpr/ppermute | solution.py:18
  264.6 7.9 %collective-permute-start = (s32[512]{0:T(512)S(1)}, s32[512]{0:T(512)S(1)}, u32[]{:S(2)}, u32[]{:S(2)}) collective-permute-start(s32[512]{0:T(512)S(1)} %get-tuple-element.152), channel_id=1, source_target_pairs={{120,0},{0,8},{8,16},{16,24},{24,32},{32,40},{40,48},{48,56},{56,6... | collective-permute-start | bytes 6152 | tf_op jit(solution)/shard_map/while/body/eval_jaxpr/ppermute | solution.py:18
  276.7 8.2 %collective-permute-start.1 = (bf16[512,1,256]{2,0,1:T(8,128)(2,1)S(1)}, bf16[512,1,256]{2,0,1:T(8,128)(2,1)S(1)}, u32[]{:S(2)}, u32[]{:S(2)}) collective-permute-start(bf16[512,1,256]{2,0,1:T(8,128)(2,1)S(1)} %get-tuple-element.151), channel_id=1, source_target_pairs={{120,0},{0,8},{8,16},{16,24},{24,32},{32,40},{40,48},{48,56},{56,6... | collective-permute-start | bytes 786440 | tf_op jit(solution)/shard_map/while/body/eval_jaxpr/ppermute | solution.py:18
  276.8 7.9 %collective-permute-start = (s32[512]{0:T(512)S(1)}, s32[512]{0:T(512)S(1)}, u32[]{:S(2)}, u32[]{:S(2)}) collective-permute-start(s32[512]{0:T(512)S(1)} %get-tuple-element.152), channel_id=1, source_target_pairs={{120,0},{0,8},{8,16},{16,24},{24,32},{32,40},{40,48},{48,56},{56,6... | collective-permute-start | bytes 6152 | tf_op jit(solution)/shard_map/while/body/eval_jaxpr/ppermute | solution.py:18
  288.8 8.2 %collective-permute-start.1 = (bf16[512,1,256]{2,0,1:T(8,128)(2,1)S(1)}, bf16[512,1,256]{2,0,1:T(8,128)(2,1)S(1)}, u32[]{:S(2)}, u32[]{:S(2)}) collective-permute-start(bf16[512,1,256]{2,0,1:T(8,128)(2,1)S(1)} %get-tuple-element.151), channel_id=1, source_target_pairs={{120,0},{0,8},{8,16},{16,24},{24,32},{32,40},{40,48},{48,56},{56,6... | collective-permute-start | bytes 786440 | tf_op jit(solution)/shard_map/while/body/eval_jaxpr/ppermute | solution.py:18
  288.9 7.9 %collective-permute-start = (s32[512]{0:T(512)S(1)}, s32[512]{0:T(512)S(1)}, u32[]{:S(2)}, u32[]{:S(2)}) collective-permute-start(s32[512]{0:T(512)S(1)} %get-tuple-element.152), channel_id=1, source_target_pairs={{120,0},{0,8},{8,16},{16,24},{24,32},{32,40},{40,48},{48,56},{56,6... | collective-permute-start | bytes 6152 | tf_op jit(solution)/shard_map/while/body/eval_jaxpr/ppermute | solution.py:18
  301.0 8.2 %collective-permute-start.1 = (bf16[512,1,256]{2,0,1:T(8,128)(2,1)S(1)}, bf16[512,1,256]{2,0,1:T(8,128)(2,1)S(1)}, u32[]{:S(2)}, u32[]{:S(2)}) collective-permute-start(bf16[512,1,256]{2,0,1:T(8,128)(2,1)S(1)} %get-tuple-element.151), channel_id=1, source_target_pairs={{120,0},{0,8},{8,16},{16,24},{24,32},{32,40},{40,48},{48,56},{56,6... | collective-permute-start | bytes 786440 | tf_op jit(solution)/shard_map/while/body/eval_jaxpr/ppermute | solution.py:18
  301.1 7.9 %collective-permute-start = (s32[512]{0:T(512)S(1)}, s32[512]{0:T(512)S(1)}, u32[]{:S(2)}, u32[]{:S(2)}) collective-permute-start(s32[512]{0:T(512)S(1)} %get-tuple-element.152), channel_id=1, source_target_pairs={{120,0},{0,8},{8,16},{16,24},{24,32},{32,40},{40,48},{48,56},{56,6... | collective-permute-start | bytes 6152 | tf_op jit(solution)/shard_map/while/body/eval_jaxpr/ppermute | solution.py:18
  (5 other events, 32.3 us)
Sparse Core Ops, SparseCore 0:
  29.9 69.4 all-gather.1
where the time goes:
time: 323 us; the launch traced here: 322 us
  waiting for transfers between devices  138 us (43%)
  matrix products  59.9 us (19%)
  local copies, waits for them, and re-layouts  55.2 us (17%)
  other arithmetic  27.7 us (9%)
  blocking collectives  22 us (7%)
  between operations  13.5 us (4%)
  starting transfers between devices  3.58 us (1%)
    ppermute x30, waiting for transfers between devices, from_behind(): return lax.ppermute(block, axis, route)  116 us
    dot_general x16, matrix products, absorb(): jnp.einsum('ghrk,kgd->ghrd', prob.astype(jnp.bfloat16), values, preferred...  30.3 us
    all_to_all x1, blocking collectives, local(): lax.all_to_all(stored_qkv, 'head', split_axis=1, concat_axis=0, tiled=True)  22 us
    all_gather x1, waiting for transfers between devices, local(): weight = lax.all_gather(mine, 'ctx', axis=0, tiled=True)  21.9 us
    gather x2, local copies, waits for them, and re-layouts, local(): tokens.reshape(rows_dev, blocks, width // blocks)[:, block_order, :]  21.2 us
    reduce_sum x16, other arithmetic, absorb(): total = total * factor + jnp.sum(prob, axis=-1)  19 us
    unnamed x18, local copies, waits for them, and re-layouts  17.8 us
    dot_general x16, matrix products, absorb(): jnp.einsum('rghd,kgd->ghrk', queries, keys, preferred_element_type=jnp.fl...  16 us
  transfers between devices with their start and end apart: 31, of which 16 were waited for; matrix products, arithmetic and copies ran while one was open for 16% of the time, Pallas kernels for 0%

commit v1 on v0

v1 whole, which is shorter than its diff:
```python
import math

import jax
import jax.numpy as jnp
from jax import lax
from jax.experimental import pallas as pl
from jax.experimental.pallas import tpu as pltpu
from jax.sharding import Mesh
from jax.sharding import PartitionSpec as P

HEAD_DIM = 128
QPG = 4
theta_base = 1000000.0

SIZES = {"zl": 2, "y": 4, "core": 2, "zh": 2, "x": 4}
CTX = ("zl", "y", "core")
HEAD = ("zh", "x")
OFFSETS = ((0, 0), (1, 0), (0, -1), (0, 1), (0, 2), (1, -1), (1, 1), (1, 2))
PIECES = len(OFFSETS)
MIB = 1024 * 1024


def shift(block, axis, distance):
    size = SIZES[axis]
    return lax.ppermute(block, axis, [(i, (i + distance) % size) for i in range(size)])


def spread(block):
    over = shift(block, "zl", 1)
    left = shift(block, "y", 1)
    right = shift(block, "y", -1)
    far = shift(block, "y", 2)
    return (
        block, over, left, right, far,
        shift(over, "y", 1), shift(over, "y", -1), shift(far, "zl", 1),
    )


def arrange_kernel(cols_ref, order_ref, a_ref, b_ref, c_ref, d_ref, out_ref):
    block = jnp.concatenate([a_ref[...], b_ref[...], c_ref[...], d_ref[...]], axis=1)
    out_ref[0] = jnp.dot(order_ref[...], block, preferred_element_type=jnp.float32).astype(
        out_ref.dtype
    )


def arrange(tokens, order, cols):
    rows, width = tokens.shape
    part = 128

    def pick(j):
        return pl.BlockSpec((rows, part), lambda p, cols_ref: (0, cols_ref[4 * p + j]))

    return pl.pallas_call(
        arrange_kernel,
        grid_spec=pltpu.PrefetchScalarGridSpec(
            num_scalar_prefetch=1,
            grid=(PIECES,),
            in_specs=[pl.BlockSpec((rows, rows), lambda p, cols_ref: (0, 0))]
            + [pick(j) for j in range(4)],
            out_specs=pl.BlockSpec((1, rows, 4 * part), lambda p, cols_ref: (p, 0, 0)),
        ),
        out_shape=jax.ShapeDtypeStruct((PIECES, rows, 4 * part), jnp.bfloat16),
        compiler_params=pltpu.CompilerParams(vmem_limit_bytes=32 * MIB),
        cost_estimate=pl.CostEstimate(
            flops=2 * rows * rows * width // 2, bytes_accessed=2 * rows * width, transcendentals=0
        ),
        name="arrange",
    )(cols, order, tokens, tokens, tokens, tokens)


def project_kernel(*refs):
    x_own, x_sib = refs[0], refs[1]
    pieces = refs[2 : 2 + PIECES]
    out_own, out_sib = refs[2 + PIECES], refs[3 + PIECES]
    x_buf, w_buf, sems = refs[4 + PIECES :]
    copies = []
    for p in range(PIECES):
        group = (
            pltpu.make_async_copy(pieces[p], w_buf.at[p], sems.at[0, p]),
            pltpu.make_async_copy(x_own.at[p], x_buf.at[0, p], sems.at[1, p]),
            pltpu.make_async_copy(x_sib.at[p], x_buf.at[1, p], sems.at[2, p]),
        )
        for copy in group:
            copy.start()
        copies.append(group)
    for p in range(PIECES):
        for copy in copies[p]:
            copy.wait()
        for half, out in enumerate((out_own, out_sib)):
            term = jnp.dot(x_buf[half, p], w_buf[p], preferred_element_type=jnp.float32)
            if p == 0:
                out[...] = term
            else:
                out[...] += term


def project(x_own, x_sib, pieces):
    rows = x_own.shape[1]
    depth, width = pieces[0].shape
    out = jax.ShapeDtypeStruct((rows, width), jnp.float32)
    return pl.pallas_call(
        project_kernel,
        in_specs=[pl.BlockSpec(memory_space=pl.ANY)] * (2 + PIECES),
        out_specs=[pl.BlockSpec(memory_space=pltpu.VMEM)] * 2,
        out_shape=[out, out],
        scratch_shapes=[
            pltpu.VMEM((2, PIECES, rows, depth), jnp.bfloat16),
            pltpu.VMEM((PIECES, depth, width), jnp.bfloat16),
            pltpu.SemaphoreType.DMA((3, PIECES)),
        ],
        compiler_params=pltpu.CompilerParams(vmem_limit_bytes=48 * MIB),
        cost_estimate=pl.CostEstimate(
            flops=4 * rows * width * depth * PIECES,
            bytes_accessed=PIECES * depth * (4 * rows + 2 * width),
            transcendentals=0,
        ),
        name="project",
    )(x_own, x_sib, *pieces)


def turn_kernel(scale, mine_ref, other_ref, bias_ref, cos_ref, sin_ref, q_ref, kv_ref):
    both = mine_ref[...] + other_ref[...] + bias_ref[...]
    cosine, sine = cos_ref[...], sin_ref[...]
    half = HEAD_DIM // 2
    for head in range(QPG + 1):
        x = both[:, head * HEAD_DIM : (head + 1) * HEAD_DIM]
        swapped = jnp.concatenate([x[:, half:], x[:, :half]], axis=1)
        y = x * cosine + swapped * sine
        if head < QPG:
            q_ref[:, head * HEAD_DIM : (head + 1) * HEAD_DIM] = (y * scale).astype(q_ref.dtype)
        else:
            kv_ref[:, :HEAD_DIM] = y.astype(kv_ref.dtype)
    kv_ref[:, HEAD_DIM:] = both[:, (QPG + 1) * HEAD_DIM :].astype(kv_ref.dtype)


def turn(mine, other, bias, cosine, sine):
    rows, width = mine.shape
    scale = math.log2(math.e) / math.sqrt(HEAD_DIM)
    return pl.pallas_call(
        lambda *refs: turn_kernel(scale, *refs),
        grid=(4,),
        in_specs=[
            pl.BlockSpec((rows // 4, width), lambda i: (i, 0)),
            pl.BlockSpec((rows // 4, width), lambda i: (i, 0)),
            pl.BlockSpec((1, width), lambda i: (0, 0)),
            pl.BlockSpec((rows // 4, HEAD_DIM), lambda i: (i, 0)),
            pl.BlockSpec((rows // 4, HEAD_DIM), lambda i: (i, 0)),
        ],
        out_specs=[
            pl.BlockSpec((rows // 4, QPG * HEAD_DIM), lambda i: (i, 0)),
            pl.BlockSpec((rows // 4, 2 * HEAD_DIM), lambda i: (i, 0)),
        ],
        out_shape=[
            jax.ShapeDtypeStruct((rows, QPG * HEAD_DIM), jnp.bfloat16),
            jax.ShapeDtypeStruct((rows, 2 * HEAD_DIM), jnp.bfloat16),
        ],
        cost_estimate=pl.CostEstimate(
            flops=4 * rows * width, bytes_accessed=10 * rows * width, transcendentals=0
        ),
        name="turn",
    )(mine, other, bias, cosine, sine)


STRIP = 64
KV_PIECES = 2 * PIECES
KEY_TILE = STRIP * KV_PIECES


def attend_kernel(full_ref, some_ref, q_ref, qpos_ref, kpos_ref, back_ref, *refs):
    pieces = refs[:KV_PIECES]
    out_ref, gathered = refs[KV_PIECES:]
    i = pl.program_id(0)
    q = jnp.concatenate(
        [q_ref[:, h * HEAD_DIM : (h + 1) * HEAD_DIM] for h in range(QPG)], axis=0
    )
    qpos = jnp.concatenate([qpos_ref[...]] * QPG, axis=0)
    ones = jnp.ones((KEY_TILE, HEAD_DIM), jnp.bfloat16)

    def absorb(masked, t, state):
        best, accum = state
        row = pl.ds(pl.multiple_of(t * STRIP, STRIP), STRIP)
        keys = jnp.concatenate([p[row, :HEAD_DIM] for p in pieces], axis=0)
        values = jnp.concatenate([p[row, HEAD_DIM:] for p in pieces], axis=0)
        values = jnp.concatenate([values, ones], axis=1)
        score = lax.dot_general(
            q, keys, (((1,), (1,)), ((), ())), preferred_element_type=jnp.float32
        )
        if masked:
            score = jnp.where(kpos_ref[t] <= qpos, score, -1e30)
        newest = jnp.maximum(best, jnp.max(score, axis=1, keepdims=True))
        prob = jnp.exp2((score - newest).astype(jnp.bfloat16))
        accum = accum * jnp.exp2(best - newest) + jnp.dot(
            prob, values, preferred_element_type=jnp.float32
        )
        return newest, accum

    state = (
        jnp.full((QPG * STRIP, 1), -1e30, jnp.float32),
        jnp.zeros((QPG * STRIP, 2 * HEAD_DIM), jnp.float32),
    )
    state = lax.fori_loop(0, full_ref[i], lambda t, s: absorb(False, t, s), state)
    _, accum = lax.fori_loop(full_ref[i], some_ref[i], lambda t, s: absorb(True, t, s), state)
    result = (accum[:, :HEAD_DIM] / accum[:, HEAD_DIM:]).astype(jnp.bfloat16)
    rows = pl.ds(pl.multiple_of(i * STRIP, STRIP), STRIP)
    for h in range(QPG):
        gathered[rows, h * HEAD_DIM : (h + 1) * HEAD_DIM] = result[h * STRIP : (h + 1) * STRIP]

    @pl.when(i == pl.num_programs(0) - 1)
    def _():
        out_ref[...] = jnp.dot(
            back_ref[...], gathered[...], preferred_element_type=jnp.float32
        ).astype(out_ref.dtype)


def attend(full, some, q, qpos, kpos, back, pieces):
    rows, width = q.shape
    tiles = kpos.shape[0]
    return pl.pallas_call(
        attend_kernel,
        grid_spec=pltpu.PrefetchScalarGridSpec(
            num_scalar_prefetch=2,
            grid=(rows // STRIP,),
            in_specs=[
                pl.BlockSpec((STRIP, width), lambda i, *_: (i, 0)),
                pl.BlockSpec((STRIP, 1), lambda i, *_: (i, 0)),
                pl.BlockSpec((tiles, 1, KEY_TILE), lambda i, *_: (0, 0, 0)),
                pl.BlockSpec((rows, rows), lambda i, *_: (0, 0)),
            ]
            + [pl.BlockSpec((rows, 2 * HEAD_DIM), lambda i, *_: (0, 0))] * KV_PIECES,
            out_specs=pl.BlockSpec((rows, width), lambda i, *_: (0, 0)),
            scratch_shapes=[pltpu.VMEM((rows, width), jnp.bfloat16)],
        ),
        out_shape=jax.ShapeDtypeStruct((rows, width), jnp.bfloat16),
        compiler_params=pltpu.CompilerParams(vmem_limit_bytes=48 * MIB),
        cost_estimate=pl.CostEstimate(
            flops=4 * rows * width * tiles * KEY_TILE // 2,
            bytes_accessed=4 * rows * KV_PIECES * HEAD_DIM,
            transcendentals=rows * QPG * tiles * KEY_TILE // 2,
        ),
        name="attend",
    )(full, some, q, qpos, kpos, back, *pieces)


def angles(positions, width):
    half = width // 2
    freq = jnp.exp(jnp.arange(half, dtype=jnp.float32) * (-2.0 * math.log(theta_base) / width))
    phase = positions.astype(jnp.float32)[:, None] * freq[None, :]
    return (jnp.cos(phase), jnp.sin(phase))


def local(tokens, positions, stored_qkv, block_order, qkv_bias):
    rows = tokens.shape[0]
    zl, y, core = (lax.axis_index(a) for a in CTX)

    rank = jnp.sum(positions[None, :] < positions[:, None], axis=1, dtype=jnp.int32)
    chosen = rank[None, :] == jnp.arange(rows, dtype=jnp.int32)[:, None]
    order = chosen.astype(jnp.bfloat16)
    back = (rank[:, None] == jnp.arange(rows, dtype=jnp.int32)[None, :]).astype(jnp.bfloat16)
    place = jnp.sum(jnp.where(chosen, positions[None, :], 0), axis=1, dtype=jnp.int32)

    def owners(which):
        return jnp.stack([(((zl + a) % 2) * 4 + (y + b) % 4) * 2 + which for a, b in OFFSETS])

    def columns(which):
        blocks = owners(which)[:, None] * 4 + jnp.arange(4, dtype=jnp.int32)[None, :]
        return block_order[blocks.reshape(-1)]

    x_away = arrange(tokens, order, columns(1 - core))
    x_sib = shift(x_away, "core", 1)
    x_own = arrange(tokens, order, columns(core))

    mine = lax.all_to_all(stored_qkv, HEAD, split_axis=1, concat_axis=0, tiled=True)
    own, away = project(x_own, x_sib, spread(mine))
    other = shift(away, "core", 1)

    cosine, sine = angles(place, HEAD_DIM)
    q, kv = turn(
        own, other, qkv_bias[None, :],
        jnp.concatenate([cosine, cosine], axis=1), jnp.concatenate([-sine, sine], axis=1),
    )

    near = spread(kv)
    pieces = near + tuple(shift(block, "core", 1) for block in near)

    every = lax.all_gather(place, CTX, axis=0, tiled=False)
    kpos = every[jnp.concatenate([owners(core), owners(1 - core)])]
    tiles = rows // STRIP
    kpos = kpos.reshape(KV_PIECES, tiles, STRIP).transpose(1, 0, 2).reshape(tiles, KEY_TILE)
    low, high = jnp.min(kpos, axis=1), jnp.max(kpos, axis=1)
    strips = place.reshape(rows // STRIP, STRIP)
    full = jnp.sum(high[None, :] <= strips[:, :1], axis=1, dtype=jnp.int32)
    some = jnp.sum(low[None, :] <= strips[:, -1:], axis=1, dtype=jnp.int32)
    return attend(full, some, q, place[:, None], kpos[:, None, :], back, pieces)


def solution(mesh):
    fine = Mesh(mesh.devices.reshape(tuple(SIZES.values())), tuple(SIZES))
    placed = (P(CTX, None), P(CTX), P(CTX + HEAD, None), P(), P(HEAD))
    return jax.shard_map(
        local, mesh=fine, in_specs=placed, out_specs=P(CTX, HEAD), check_vma=False
    )
```

time: 323 us -> 200 us (0.62)
  waiting for transfers between devices: 138 us -> 40.5 us
  Pallas kernels: 0 us -> 68.5 us
  matrix products: 59.9 us -> 0 us
  local copies, waits for them, and re-layouts: 55.2 us -> 16.8 us
  other arithmetic: 27.7 us -> 4.18 us
  blocking collectives: 22 us -> 44 us
  starting transfers between devices: 3.58 us -> 24.6 us
  between operations: 13.5 us -> 0.2 us
    ppermute x30 -> x24, waiting for transfers between devices: 116 us -> 40.5 us  [shift(): lax.ppermute(block, axis, [(i, (i + distance) % size) for i in range(size)])]
    pallas_call x0 -> x5, Pallas kernels: none -> 68.5 us  [the longest x1 41.7 us: attend(): pl.pallas_call(attend_kernel, grid_spec=pltpu.PrefetchScalarGridSpec(num_...]
    dot_general x33 -> x0, matrix products: 59.9 us -> none  [the longest x16 30.3 us: absorb(): jnp.einsum('ghrk,kgd->ghrd', prob.astype(jnp.bfloat16), values, preferred...]
    all_gather x1 -> x0, waiting for transfers between devices: 21.9 us -> none  [local(): weight = lax.all_gather(mine, 'ctx', axis=0, tiled=True)]
    all_gather x0 -> x1, blocking collectives: none -> 21.5 us  [local(): every = lax.all_gather(place, CTX, axis=0, tiled=False)]
    ppermute x30 -> x24, starting transfers between devices: 3.58 us -> 24.6 us  [shift(): lax.ppermute(block, axis, [(i, (i + distance) % size) for i in range(size)])]
    gather x2 -> x3, local copies, waits for them, and re-layouts: 21.2 us -> 1.97 us  [the longest x2 1.4 us: columns(): return block_order[blocks.reshape(-1)]]
    reduce_sum x16 -> x3, other arithmetic: 19 us -> 1.41 us  [the longest x1 1.01 us: local(): jnp.sum(positions[None, :] < positions[:, None], axis=1, dtype=jnp.int32)]
  transfers between devices with their start and end apart: 31 -> 24, of which waited for: 16 -> 10; matrix products, arithmetic and copies ran while one was open for 16% -> 3% of each run, Pallas kernels for 0% -> 3%
where the time goes in v1:
time: 200 us; the launch traced here: 199 us
  Pallas kernels  68.5 us (34%)
  blocking collectives  44 us (22%)
  waiting for transfers between devices  40.5 us (20%)
  starting transfers between devices  24.6 us (12%)
  local copies, waits for them, and re-layouts  16.8 us (8%)
  other arithmetic  4.18 us (2%)
    pallas_call x1, Pallas kernels, attend(): pl.pallas_call(attend_kernel, grid_spec=pltpu.PrefetchScalarGridSpec(num_...  41.7 us
    ppermute x24, waiting for transfers between devices, shift(): lax.ppermute(block, axis, [(i, (i + distance) % size) for i in range(size)])  40.5 us
    ppermute x24, starting transfers between devices, shift(): lax.ppermute(block, axis, [(i, (i + distance) % size) for i in range(size)])  24.6 us
    all_to_all x1, blocking collectives, local(): lax.all_to_all(stored_qkv, HEAD, split_axis=1, concat_axis=0, tiled=True)  22.6 us
    all_gather x1, blocking collectives, local(): every = lax.all_gather(place, CTX, axis=0, tiled=False)  21.5 us
    unnamed x25, local copies, waits for them, and re-layouts  13 us
    pallas_call x2, Pallas kernels, arrange(): pl.pallas_call(arrange_kernel, grid_spec=pltpu.PrefetchScalarGridSpec(num...  12.5 us
    pallas_call x1, Pallas kernels, project(): pl.pallas_call(project_kernel, in_specs=[pl.BlockSpec(memory_space=pl.ANY...  10.3 us
  transfers between devices with their start and end apart: 24, of which 10 were waited for; matrix products, arithmetic and copies ran while one was open for 3% of the time, Pallas kernels for 3%

profile of v1, /device:TPU:0, one launch (start us, length us, event | category | flops | bytes accessed | tf_op | source)
XLA Modules:
  0.0 198.9 jit_solution(18430724562978549324)
XLA Ops:
  0.3 1.0 convert_reduce_fusion
  2.3 3.4 %copy-done.1 = bf16[512,8192]{1,0:T(8,128)(2,1)S(1)} copy-done((bf16[512,8192]{1,0:T(8,128)(2,1)S(1)}, bf16[512,8192]{1,0:T(8,128)(2,1)}, u32[]{:S(2)}) %copy-start.1) | copy-done | bytes 8388632
  5.7 6.9 %arrange.3 = bf16[8,512,512]{2,1,0:T(8,128)(2,1)} custom-call(s32[32]{0:T(128)S(1)} %gather_fusion.2, bf16[512,512]{1,0:T(8,128)(2,1)S(1)} %get-tuple-element.21.order_ref, bf16[512,8192]{1,0:T(8,128)(2,1)S(1)} %copy-done.1, bf16[512,8192]{1,0:T(8,128)(2,1)S(1)} %copy-done.1, bf16[512,8192]{1,0:T(8,128)(2,1)S(1)} %copy-done.1, bf16[512,8192]{1,0:T(8,128)(2,1)S(1)} %copy-done.1), custom_call_target="tpu_custom_call" | custom-call | flops 2147483648 | bytes 8388608 | tf_op jit(solution)/shard_map/arrange/pallas_call | solution.py:53
  12.6 22.6 %all_to_all.19 = bf16[64,8,768]{2,0,1:T(8,128)(2,1)S(1)} all-to-all(bf16[64,8,768]{2,0,1:T(8,128)(2,1)S(1)} %bitcast.58), channel_id=1, replica_groups=mesh['zl'=2,'y'=4,'core'=2,'zh'=2,'x'=4] {'zh','x'}, dimensions={1} | all-to-all | bytes 1572864 | tf_op jit(solution)/shard_map/all_to_all | solution.py:272
  35.2 1.0 collective-permute-start.1
  36.2 3.2 %collective-permute-start.4 = (bf16[512,768]{1,0:T(8,128)(2,1)S(1)}, bf16[512,768]{1,0:T(8,128)(2,1)S(1)}, u32[]{:S(2)}, u32[]{:S(2)}) collective-permute-start(bf16[512,768]{1,0:T(8,128)(2,1)S(1)} %bitcast.54), channel_id=1, source_target_pairs={{0,32},{16,48},{32,0},{48,16},{1,33},{17,49},{33,1},{49,17},{2,34}... | collective-permute-start | bytes 2359304 | tf_op jit(solution)/shard_map/ppermute | solution.py:25
  40.2 2.6 %collective-permute-start.3 = (bf16[512,768]{1,0:T(8,128)(2,1)S(1)}, bf16[512,768]{1,0:T(8,128)(2,1)}, u32[]{:S(2)}, u32[]{:S(2)}) collective-permute-start(bf16[512,768]{1,0:T(8,128)(2,1)S(1)} %bitcast.56), channel_id=1, source_target_pairs={{0,48},{16,0},{32,16},{48,32},{1,49},{17,1},{33,17},{49,33},{2,50}... | collective-permute-start | bytes 2359304 | tf_op jit(solution)/shard_map/ppermute | solution.py:25
  42.7 11.6 %collective-permute-done.1.refs_3_ = bf16[512,768]{1,0:T(8,128)(2,1)S(1)} collective-permute-done((bf16[512,768]{1,0:T(8,128)(2,1)S(1)}, bf16[512,768]{1,0:T(8,128)(2,1)S(1)}, u32[]{:S(2)}, u32[]{:S(2)}) %collective-permute-start.1) | collective-permute-done | bytes 786464 | tf_op jit(solution)/shard_map/ppermute | solution.py:25
  54.3 1.6 collective-permute-start.5
  55.9 2.3 %collective-permute-done.4.refs_6_ = bf16[512,768]{1,0:T(8,128)(2,1)S(1)} collective-permute-done((bf16[512,768]{1,0:T(8,128)(2,1)S(1)}, bf16[512,768]{1,0:T(8,128)(2,1)S(1)}, u32[]{:S(2)}, u32[]{:S(2)}) %collective-permute-start.4) | collective-permute-done | bytes 786464 | tf_op jit(solution)/shard_map/ppermute | solution.py:25
  58.2 3.0 %collective-permute-start.6 = (bf16[512,768]{1,0:T(8,128)(2,1)S(1)}, bf16[512,768]{1,0:T(8,128)(2,1)}, u32[]{:S(2)}, u32[]{:S(2)}) collective-permute-start(bf16[512,768]{1,0:T(8,128)(2,1)S(1)} %collective-permute-done.1.refs_3_), channel_id=1, source_target_pairs={{0,48},{16,0},{32,16},{48,32},{1,49},{17,1},{33,17},{49,33},{2,50}... | collective-permute-start | bytes 2359304 | tf_op jit(solution)/shard_map/ppermute | solution.py:25
  61.3 13.0 %collective-permute-done.2.refs_4_ = bf16[512,768]{1,0:T(8,128)(2,1)} collective-permute-done((bf16[512,768]{1,0:T(8,128)(2,1)S(1)}, bf16[512,768]{1,0:T(8,128)(2,1)}, u32[]{:S(2)}, u32[]{:S(2)}) %collective-permute-start.2) | collective-permute-done | bytes 786464 | tf_op jit(solution)/shard_map/ppermute | solution.py:25
  74.3 1.0 collective-permute-start.7
  76.1 3.4 %copy-done.2 = bf16[512,8192]{1,0:T(8,128)(2,1)S(1)} copy-done((bf16[512,8192]{1,0:T(8,128)(2,1)S(1)}, bf16[512,8192]{1,0:T(8,128)(2,1)}, u32[]{:S(2)}) %copy-start.2) | copy-done | bytes 8388632
  79.5 5.6 %arrange.2.refs_0_ = bf16[8,512,512]{2,1,0:T(8,128)(2,1)S(1)} custom-call(s32[32]{0:T(128)S(1)} %gather_fusion.1, bf16[512,512]{1,0:T(8,128)(2,1)S(1)} %get-tuple-element.21.order_ref, bf16[512,8192]{1,0:T(8,128)(2,1)S(1)} %copy-done.2, bf16[512,8192]{1,0:T(8,128)(2,1)S(1)} %copy-done.2, bf16[512,8192]{1,0:T(8,128)(2,1)S(1)} %copy-done.2, ...), custom_call_target="tpu_custom_call" | custom-call | flops 2147483648 | bytes 8388608 | tf_op jit(solution)/shard_map/arrange/pallas_call | solution.py:53
  85.1 2.0 copy-done.3
  87.1 3.3 %collective-permute-done.5.refs_7_ = bf16[512,768]{1,0:T(8,128)(2,1)} collective-permute-done((bf16[512,768]{1,0:T(8,128)(2,1)S(1)}, bf16[512,768]{1,0:T(8,128)(2,1)}, u32[]{:S(2)}, u32[]{:S(2)}) %collective-permute-start.5) | collective-permute-done | bytes 786464 | tf_op jit(solution)/shard_map/ppermute | solution.py:25
  90.8 2.3 %collective-permute-done.7.refs_9_ = bf16[512,768]{1,0:T(8,128)(2,1)} collective-permute-done((bf16[512,768]{1,0:T(8,128)(2,1)S(1)}, bf16[512,768]{1,0:T(8,128)(2,1)}, u32[]{:S(2)}, u32[]{:S(2)}) %collective-permute-start.7) | collective-permute-done | bytes 786464 | tf_op jit(solution)/shard_map/ppermute | solution.py:25
  93.1 10.3 %project.1 = (f32[512,768]{1,0:T(8,128)}, f32[512,768]{1,0:T(8,128)}) custom-call(bf16[8,512,512]{2,1,0:T(8,128)(2,1)} %copy-done.3, bf16[8,512,512]{2,1,0:T(8,128)(2,1)} %collective-permute-done.refs_1_, bf16[512,768]{1,0:T(8,128)(2,1)S(1)} %bitcast.57, bf16[512,768]{1,0:T(8,128)(2,1)S(1)} %collective-permute-done.1.refs_3_, ...), custom_call_target="tpu_custom_call" | custom-call | flops 6442450944 | bytes 14680064 | tf_op jit(solution)/shard_map/project/pallas_call | solution.py:101
  107.1 1.2 copy-done.8
  108.3 4.0 %turn.1 = (bf16[512,512]{1,0:T(8,128)(2,1)}, bf16[512,256]{1,0:T(8,128)(2,1)}) custom-call(f32[512,768]{1,0:T(8,128)} %get-tuple-element.9.refs_0_, f32[512,768]{1,0:T(8,128)} %copy-done.8, f32[1,768]{1,0:T(1,128)} %broadcast_in_dim.9.refs_2_, f32[512,128]{1,0:T(8,128)} %get-tuple-element.24.refs_3_, f32[512,128]{1,0:T(8,128)} %get-tuple-element.25.refs_4_), custom_call_target="tpu_custom_call" | custom-call | flops 1572864 | bytes 3932160 | tf_op jit(solution)/shard_map/turn/pallas_call | solution.py:139
  112.3 1.0 collective-permute-start.9
  113.4 1.6 collective-permute-start.12
  114.9 3.2 %collective-permute-start.11 = (bf16[512,256]{1,0:T(8,128)(2,1)}, bf16[512,256]{1,0:T(8,128)(2,1)S(1)}, u32[]{:S(2)}, u32[]{:S(2)}) collective-permute-start(bf16[512,256]{1,0:T(8,128)(2,1)} %get-tuple-element.12.refs_0_), channel_id=1, source_target_pairs={{0,48},{16,0},{32,16},{48,32},{1,49},{17,1},{33,17},{49,33},{2,50}... | collective-permute-start | bytes 786440 | tf_op jit(solution)/shard_map/ppermute | solution.py:25
  118.2 21.5 %all-gather.1 = s32[16,1,512]{2,1,0:T(1,128)S(1)} all-gather(s32[1,1,512]{2,1,0:T(1,128)S(1)} %bitcast.62), channel_id=2, replica_groups=mesh['zl'=2,'y'=4,'core'=2,'zh'=2,'x'=4] {'zl','y','core'}, dimensions={0}, use_global_device_ids=true | all-gather | bytes 34816 | tf_op jit(solution)/shard_map/all_gather | solution.py:285
  139.8 1.3 collective-permute-start.13
  141.1 2.0 collective-permute-start.14
  143.1 1.1 collective-permute-start.15
  144.9 4.7 %collective-permute-done.13.refs_5_ = bf16[512,256]{1,0:T(8,128)(2,1)S(1)} collective-permute-done((bf16[512,256]{1,0:T(8,128)(2,1)S(1)}, bf16[512,256]{1,0:T(8,128)(2,1)S(1)}, u32[]{:S(2)}, u32[]{:S(2)}) %collective-permute-start.13) | collective-permute-done | bytes 262176 | tf_op jit(solution)/shard_map/ppermute | solution.py:25
  150.1 1.7 collective-permute-done.15.refs_7_
  154.2 1.0 copy-done.4
  157.2 41.7 %attend.1 = bf16[512,512]{1,0:T(8,128)(2,1)} custom-call(s32[8]{0:T(128)S(1)} %get-tuple-element.23.full_ref, s32[8]{0:T(128)S(1)} %get-tuple-element.22.some_ref, bf16[512,512]{1,0:T(8,128)(2,1)S(1)} %copy-done.4, s32[512,1]{1,0:T(8,128)S(1)} %copy.19.qpos_ref, s32[8,1,1024]{2,1,0:T(1,128)S(1)} %broadcast_in_dim_reshape.3.kpos_ref, ...), custom_call_target="tpu_custom_call" | custom-call | flops 4294967296 | bytes 4194304 | tf_op jit(solution)/shard_map/attend/pallas_call | solution.py:218
  (87 shorter events, 12.7 us)
Async XLA Ops:
  0.0 1.6 copy-start
  2.3 3.4 %copy-start.1 = (bf16[512,8192]{1,0:T(8,128)(2,1)S(1)}, bf16[512,8192]{1,0:T(8,128)(2,1)}, u32[]{:S(2)}) copy-start(bf16[512,8192]{1,0:T(8,128)(2,1)} %d_ref.3) | copy-start | bytes 25165828
  5.7 6.9 %copy-start.9 = (bf16[64,6144]{1,0:T(8,128)(2,1)S(1)}, bf16[64,6144]{1,0:T(8,128)(2,1)}, u32[]{:S(2)}) copy-start(bf16[64,6144]{1,0:T(8,128)(2,1)} %param.7) | copy-start | bytes 2359300
  12.6 80.6 %collective-permute-start = (bf16[8,512,512]{2,1,0:T(8,128)(2,1)}, bf16[8,512,512]{2,1,0:T(8,128)(2,1)}, u32[]{:S(2)}, u32[]{:S(2)}) collective-permute-start(bf16[8,512,512]{2,1,0:T(8,128)(2,1)} %arrange.3), channel_id=1, source_target_pairs={{0,8},{8,0},{1,9},{9,1},{2,10},{10,2},{3,11},{11,3},{4,12},{12,4},... | collective-permute-start | bytes 12582920 | tf_op jit(solution)/shard_map/ppermute | solution.py:25
  35.2 19.2 %collective-permute-start.1 = (bf16[512,768]{1,0:T(8,128)(2,1)S(1)}, bf16[512,768]{1,0:T(8,128)(2,1)S(1)}, u32[]{:S(2)}, u32[]{:S(2)}) collective-permute-start(bf16[512,768]{1,0:T(8,128)(2,1)S(1)} %bitcast.53), channel_id=1, source_target_pairs={{0,64},{64,0},{1,65},{65,1},{2,66},{66,2},{3,67},{67,3},{4,68},{68... | collective-permute-start | bytes 2359304 | tf_op jit(solution)/shard_map/ppermute | solution.py:25
  36.2 22.0 %collective-permute-start.4 = (bf16[512,768]{1,0:T(8,128)(2,1)S(1)}, bf16[512,768]{1,0:T(8,128)(2,1)S(1)}, u32[]{:S(2)}, u32[]{:S(2)}) collective-permute-start(bf16[512,768]{1,0:T(8,128)(2,1)S(1)} %bitcast.54), channel_id=1, source_target_pairs={{0,32},{16,48},{32,0},{48,16},{1,33},{17,49},{33,1},{49,17},{2,34}... | collective-permute-start | bytes 2359304 | tf_op jit(solution)/shard_map/ppermute | solution.py:25
  39.4 34.9 %collective-permute-start.2 = (bf16[512,768]{1,0:T(8,128)(2,1)S(1)}, bf16[512,768]{1,0:T(8,128)(2,1)}, u32[]{:S(2)}, u32[]{:S(2)}) collective-permute-start(bf16[512,768]{1,0:T(8,128)(2,1)S(1)} %bitcast.55), channel_id=1, source_target_pairs={{0,16},{16,32},{32,48},{48,0},{1,17},{17,33},{33,49},{49,1},{2,18}... | collective-permute-start | bytes 2359304 | tf_op jit(solution)/shard_map/ppermute | solution.py:25
  40.2 46.9 %collective-permute-start.3 = (bf16[512,768]{1,0:T(8,128)(2,1)S(1)}, bf16[512,768]{1,0:T(8,128)(2,1)}, u32[]{:S(2)}, u32[]{:S(2)}) collective-permute-start(bf16[512,768]{1,0:T(8,128)(2,1)S(1)} %bitcast.56), channel_id=1, source_target_pairs={{0,48},{16,0},{32,16},{48,32},{1,49},{17,1},{33,17},{49,33},{2,50}... | collective-permute-start | bytes 2359304 | tf_op jit(solution)/shard_map/ppermute | solution.py:25
  54.3 36.1 %collective-permute-start.5 = (bf16[512,768]{1,0:T(8,128)(2,1)S(1)}, bf16[512,768]{1,0:T(8,128)(2,1)}, u32[]{:S(2)}, u32[]{:S(2)}) collective-permute-start(bf16[512,768]{1,0:T(8,128)(2,1)S(1)} %collective-permute-done.1.refs_3_), channel_id=1, source_target_pairs={{0,16},{16,32},{32,48},{48,0},{1,17},{17,33},{33,49},{49,1},{2,18}... | collective-permute-start | bytes 2359304 | tf_op jit(solution)/shard_map/ppermute | solution.py:25
  58.2 32.5 %collective-permute-start.6 = (bf16[512,768]{1,0:T(8,128)(2,1)S(1)}, bf16[512,768]{1,0:T(8,128)(2,1)}, u32[]{:S(2)}, u32[]{:S(2)}) collective-permute-start(bf16[512,768]{1,0:T(8,128)(2,1)S(1)} %collective-permute-done.1.refs_3_), channel_id=1, source_target_pairs={{0,48},{16,0},{32,16},{48,32},{1,49},{17,1},{33,17},{49,33},{2,50}... | collective-permute-start | bytes 2359304 | tf_op jit(solution)/shard_map/ppermute | solution.py:25
  74.3 18.9 %collective-permute-start.7 = (bf16[512,768]{1,0:T(8,128)(2,1)S(1)}, bf16[512,768]{1,0:T(8,128)(2,1)}, u32[]{:S(2)}, u32[]{:S(2)}) collective-permute-start(bf16[512,768]{1,0:T(8,128)(2,1)S(1)} %collective-permute-done.4.refs_6_), channel_id=1, source_target_pairs={{0,64},{64,0},{1,65},{65,1},{2,66},{66,2},{3,67},{67,3},{4,68},{68... | collective-permute-start | bytes 2359304 | tf_op jit(solution)/shard_map/ppermute | solution.py:25
  76.1 3.4 %copy-start.2 = (bf16[512,8192]{1,0:T(8,128)(2,1)S(1)}, bf16[512,8192]{1,0:T(8,128)(2,1)}, u32[]{:S(2)}) copy-start(bf16[512,8192]{1,0:T(8,128)(2,1)} %d_ref.3) | copy-start | bytes 25165828
  85.1 2.0 copy-start.3
  87.1 16.4 %copy-start.10 = (s32[512]{0:T(512)S(1)}, s32[512]{0:T(512)}, u32[]{:S(2)}) copy-start(s32[512]{0:T(512)} %param.6) | copy-start | bytes 6148
  87.1 16.6 %copy-start.11 = (f32[768]{0:T(1024)S(1)}, f32[768]{0:T(1024)}, u32[]{:S(2)}) copy-start(f32[768]{0:T(1024)} %param.9) | copy-start | bytes 9220
  103.4 3.7 %collective-permute-start.8 = (f32[512,768]{1,0:T(8,128)}, f32[512,768]{1,0:T(8,128)S(1)}, u32[]{:S(2)}, u32[]{:S(2)}) collective-permute-start(f32[512,768]{1,0:T(8,128)} %get-tuple-element.10), channel_id=1, source_target_pairs={{0,8},{8,0},{1,9},{9,1},{2,10},{10,2},{3,11},{11,3},{4,12},{12,4},... | collective-permute-start | bytes 4718600 | tf_op jit(solution)/shard_map/ppermute | solution.py:25
  107.1 1.2 copy-start.8
  112.3 27.4 %collective-permute-start.9 = (bf16[512,256]{1,0:T(8,128)(2,1)}, bf16[512,256]{1,0:T(8,128)(2,1)S(1)}, u32[]{:S(2)}, u32[]{:S(2)}) collective-permute-start(bf16[512,256]{1,0:T(8,128)(2,1)} %get-tuple-element.12.refs_0_), channel_id=1, source_target_pairs={{0,64},{64,0},{1,65},{65,1},{2,66},{66,2},{3,67},{67,3},{4,68},{68... | collective-permute-start | bytes 786440 | tf_op jit(solution)/shard_map/ppermute | solution.py:25
  113.4 27.8 %collective-permute-start.12 = (bf16[512,256]{1,0:T(8,128)(2,1)}, bf16[512,256]{1,0:T(8,128)(2,1)S(1)}, u32[]{:S(2)}, u32[]{:S(2)}) collective-permute-start(bf16[512,256]{1,0:T(8,128)(2,1)} %get-tuple-element.12.refs_0_), channel_id=1, source_target_pairs={{0,32},{16,48},{32,0},{48,16},{1,33},{17,49},{33,1},{49,17},{2,34}... | collective-permute-start | bytes 786440 | tf_op jit(solution)/shard_map/ppermute | solution.py:25
  114.9 28.2 %collective-permute-start.10 = (bf16[512,256]{1,0:T(8,128)(2,1)}, bf16[512,256]{1,0:T(8,128)(2,1)S(1)}, u32[]{:S(2)}, u32[]{:S(2)}) collective-permute-start(bf16[512,256]{1,0:T(8,128)(2,1)} %get-tuple-element.12.refs_0_), channel_id=1, source_target_pairs={{0,16},{16,32},{32,48},{48,0},{1,17},{17,33},{33,49},{49,1},{2,18}... | collective-permute-start | bytes 786440 | tf_op jit(solution)/shard_map/ppermute | solution.py:25
  114.9 28.2 %collective-permute-start.11 = (bf16[512,256]{1,0:T(8,128)(2,1)}, bf16[512,256]{1,0:T(8,128)(2,1)S(1)}, u32[]{:S(2)}, u32[]{:S(2)}) collective-permute-start(bf16[512,256]{1,0:T(8,128)(2,1)} %get-tuple-element.12.refs_0_), channel_id=1, source_target_pairs={{0,48},{16,0},{32,16},{48,32},{1,49},{17,1},{33,17},{49,33},{2,50}... | collective-permute-start | bytes 786440 | tf_op jit(solution)/shard_map/ppermute | solution.py:25
  118.2 26.0 %collective-permute-start.16 = (bf16[512,256]{1,0:T(8,128)(2,1)}, bf16[512,256]{1,0:T(8,128)(2,1)S(1)}, u32[]{:S(2)}, u32[]{:S(2)}) collective-permute-start(bf16[512,256]{1,0:T(8,128)(2,1)} %get-tuple-element.12.refs_0_), channel_id=1, source_target_pairs={{0,8},{8,0},{1,9},{9,1},{2,10},{10,2},{3,11},{11,3},{4,12},{12,4},... | collective-permute-start | bytes 786440 | tf_op jit(solution)/shard_map/ppermute | solution.py:25
  139.8 9.8 %collective-permute-start.13 = (bf16[512,256]{1,0:T(8,128)(2,1)S(1)}, bf16[512,256]{1,0:T(8,128)(2,1)S(1)}, u32[]{:S(2)}, u32[]{:S(2)}) collective-permute-start(bf16[512,256]{1,0:T(8,128)(2,1)S(1)} %collective-permute-done.9.refs_1_), channel_id=1, source_target_pairs={{0,16},{16,32},{32,48},{48,0},{1,17},{17,33},{33,49},{49,1},{2,18}... | collective-permute-start | bytes 786440 | tf_op jit(solution)/shard_map/ppermute | solution.py:25
  141.1 8.5 %collective-permute-start.14 = (bf16[512,256]{1,0:T(8,128)(2,1)S(1)}, bf16[512,256]{1,0:T(8,128)(2,1)S(1)}, u32[]{:S(2)}, u32[]{:S(2)}) collective-permute-start(bf16[512,256]{1,0:T(8,128)(2,1)S(1)} %collective-permute-done.9.refs_1_), channel_id=1, source_target_pairs={{0,48},{16,0},{32,16},{48,32},{1,49},{17,1},{33,17},{49,33},{2,50}... | collective-permute-start | bytes 786440 | tf_op jit(solution)/shard_map/ppermute | solution.py:25
  143.1 8.7 %collective-permute-start.17 = (bf16[512,256]{1,0:T(8,128)(2,1)S(1)}, bf16[512,256]{1,0:T(8,128)(2,1)S(1)}, u32[]{:S(2)}, u32[]{:S(2)}) collective-permute-start(bf16[512,256]{1,0:T(8,128)(2,1)S(1)} %collective-permute-done.9.refs_1_), channel_id=1, source_target_pairs={{0,8},{8,0},{1,9},{9,1},{2,10},{10,2},{3,11},{11,3},{4,12},{12,4},... | collective-permute-start | bytes 786440 | tf_op jit(solution)/shard_map/ppermute | solution.py:25
  143.1 8.7 %collective-permute-start.15 = (bf16[512,256]{1,0:T(8,128)(2,1)S(1)}, bf16[512,256]{1,0:T(8,128)(2,1)S(1)}, u32[]{:S(2)}, u32[]{:S(2)}) collective-permute-start(bf16[512,256]{1,0:T(8,128)(2,1)S(1)} %collective-permute-done.12.refs_4_), channel_id=1, source_target_pairs={{0,64},{64,0},{1,65},{65,1},{2,66},{66,2},{3,67},{67,3},{4,68},{68... | collective-permute-start | bytes 786440 | tf_op jit(solution)/shard_map/ppermute | solution.py:25
  144.2 8.1 %collective-permute-start.18 = (bf16[512,256]{1,0:T(8,128)(2,1)S(1)}, bf16[512,256]{1,0:T(8,128)(2,1)S(1)}, u32[]{:S(2)}, u32[]{:S(2)}) collective-permute-start(bf16[512,256]{1,0:T(8,128)(2,1)S(1)} %collective-permute-done.10.refs_2_), channel_id=1, source_target_pairs={{0,8},{8,0},{1,9},{9,1},{2,10},{10,2},{3,11},{11,3},{4,12},{12,4},... | collective-permute-start | bytes 786440 | tf_op jit(solution)/shard_map/ppermute | solution.py:25
  149.6 4.3 %collective-permute-start.20 = (bf16[512,256]{1,0:T(8,128)(2,1)S(1)}, bf16[512,256]{1,0:T(8,128)(2,1)}, u32[]{:S(2)}, u32[]{:S(2)}) collective-permute-start(bf16[512,256]{1,0:T(8,128)(2,1)S(1)} %collective-permute-done.12.refs_4_), channel_id=1, source_target_pairs={{0,8},{8,0},{1,9},{9,1},{2,10},{10,2},{3,11},{11,3},{4,12},{12,4},... | collective-permute-start | bytes 786440 | tf_op jit(solution)/shard_map/ppermute | solution.py:25
  149.6 4.2 %collective-permute-start.19 = (bf16[512,256]{1,0:T(8,128)(2,1)S(1)}, bf16[512,256]{1,0:T(8,128)(2,1)}, u32[]{:S(2)}, u32[]{:S(2)}) collective-permute-start(bf16[512,256]{1,0:T(8,128)(2,1)S(1)} %collective-permute-done.11.refs_3_), channel_id=1, source_target_pairs={{0,8},{8,0},{1,9},{9,1},{2,10},{10,2},{3,11},{11,3},{4,12},{12,4},... | collective-permute-start | bytes 786440 | tf_op jit(solution)/shard_map/ppermute | solution.py:25
  151.8 2.0 %collective-permute-start.21 = (bf16[512,256]{1,0:T(8,128)(2,1)S(1)}, bf16[512,256]{1,0:T(8,128)(2,1)}, u32[]{:S(2)}, u32[]{:S(2)}) collective-permute-start(bf16[512,256]{1,0:T(8,128)(2,1)S(1)} %collective-permute-done.13.refs_5_), channel_id=1, source_target_pairs={{0,8},{8,0},{1,9},{9,1},{2,10},{10,2},{3,11},{11,3},{4,12},{12,4},... | collective-permute-start | bytes 786440 | tf_op jit(solution)/shard_map/ppermute | solution.py:25
  151.8 2.0 %collective-permute-start.22 = (bf16[512,256]{1,0:T(8,128)(2,1)S(1)}, bf16[512,256]{1,0:T(8,128)(2,1)}, u32[]{:S(2)}, u32[]{:S(2)}) collective-permute-start(bf16[512,256]{1,0:T(8,128)(2,1)S(1)} %collective-permute-done.14.refs_6_), channel_id=1, source_target_pairs={{0,8},{8,0},{1,9},{9,1},{2,10},{10,2},{3,11},{11,3},{4,12},{12,4},... | collective-permute-start | bytes 786440 | tf_op jit(solution)/shard_map/ppermute | solution.py:25
  152.3 1.9 collective-permute-start.23
  (4 other events, 3.7 us)

commit v2 on v0

v2 whole, which is shorter than its diff:
```python
import functools
import math

import jax
import jax.numpy as jnp
from jax import lax
from jax.experimental import pallas as pl
from jax.experimental.pallas import tpu as pltpu
from jax.sharding import Mesh
from jax.sharding import PartitionSpec as P

HEAD_DIM = 128
QPG = 4
theta_base = 1000000.0

SIZES = {"zl": 2, "y": 4, "core": 2, "zh": 2, "x": 4}
CTX = ("zl", "y", "core")
HEAD = ("zh", "x")
OFFSETS = ((0, 0), (1, 0), (0, -1), (0, 1), (0, 2), (1, -1), (1, 1), (1, 2))
PIECES = len(OFFSETS)
MIB = 1024 * 1024
SMALL = pl.CostEstimate(flops=1, bytes_accessed=1, transcendentals=0)


def shift(block, axis, distance):
    size = SIZES[axis]
    return lax.ppermute(block, axis, [(i, (i + distance) % size) for i in range(size)])


def second(over, far):
    return far, shift(over, "y", 1), shift(over, "y", -1), shift(far, "zl", 1)


def after_kernel(*refs):
    del refs


def after(arrays, *tokens):
    count = len(arrays)
    return pl.pallas_call(
        after_kernel,
        in_specs=[pl.BlockSpec(memory_space=pl.ANY)] * (count + len(tokens)),
        out_specs=[pl.BlockSpec(memory_space=pl.ANY)] * count,
        out_shape=[jax.ShapeDtypeStruct(a.shape, a.dtype) for a in arrays],
        input_output_aliases={i: i for i in range(count)},
        cost_estimate=SMALL,
        name="after",
    )(*arrays, *tokens)


def split_kernel(start, place_ref, own_ref, got_ref, token_ref, *outs):
    zh, x = place_ref[0], place_ref[1]
    rows, width = outs[0].shape[0] // 2, outs[0].shape[1]
    heads = SIZES["x"]
    span = own_ref.shape[1] // (SIZES["zh"] * heads)
    for d, out in enumerate(outs):
        head = lax.rem(x + d, heads)
        here = pl.multiple_of((zh * heads + head) * span + start, 128)
        there = pl.multiple_of(head * width, 128)
        out[pl.ds(pl.multiple_of(zh * rows, 64), rows), :] = own_ref[:, pl.ds(here, width)]
        out[pl.ds(pl.multiple_of((1 - zh) * rows, 64), rows), :] = got_ref[:, pl.ds(there, width)]


def split(place, own, got, token, start, width):
    whole = pl.BlockSpec(memory_space=pltpu.VMEM)
    return pl.pallas_call(
        functools.partial(split_kernel, start),
        in_specs=[
            pl.BlockSpec(memory_space=pltpu.SMEM), whole, whole, pl.BlockSpec(memory_space=pl.ANY),
        ],
        out_specs=[whole] * SIZES["x"],
        out_shape=[jax.ShapeDtypeStruct((2 * own.shape[0], width), own.dtype)] * SIZES["x"],
        cost_estimate=SMALL,
        name="split",
    )(place, own, got, token)


def merge_kernel(place_ref, *refs):
    x = place_ref[1]
    heads = SIZES["x"]
    out_ref = refs[-1]
    rows = refs[0].shape[0] // 2
    for d in range(heads):
        source = lax.rem(x + heads - d, heads)
        for side in range(2):
            to = pl.ds(pl.multiple_of((side * heads + source) * rows, 64), rows)
            out_ref[to, :] = refs[d][side * rows : (side + 1) * rows, :]


def merge(place, blocks, *tokens):
    rows, width = blocks[0].shape
    whole = pl.BlockSpec(memory_space=pltpu.VMEM)
    return pl.pallas_call(
        merge_kernel,
        in_specs=[pl.BlockSpec(memory_space=pltpu.SMEM)]
        + [whole] * len(blocks)
        + [pl.BlockSpec(memory_space=pl.ANY)] * len(tokens),
        out_specs=whole,
        out_shape=jax.ShapeDtypeStruct((len(blocks) * rows, width), blocks[0].dtype),
        cost_estimate=SMALL,
        name="merge",
    )(place, *blocks, *tokens)


DEPTH = 4
BLOCK = 128


def project_kernel(pieces, skip, cols_ref, x_own, x_sib, *refs):
    weights = refs[:pieces]
    refs = refs[pieces + 1 :]
    before = refs[:2] if skip else (None, None)
    if skip:
        refs = refs[2:]
    outs = refs[:2]
    x_buf, w_buf, sems = refs[2:]
    copies = []
    for p in range(pieces):
        group = [pltpu.make_async_copy(weights[p], w_buf.at[p], sems.at[2 * DEPTH, p])]
        for j in range(DEPTH):
            column = pl.multiple_of(cols_ref[(p + skip) * DEPTH + j] * BLOCK, BLOCK)
            for half, source in enumerate((x_own, x_sib)):
                group.append(
                    pltpu.make_async_copy(
                        source.at[:, pl.ds(column, BLOCK)],
                        x_buf.at[half, p, :, pl.ds(j * BLOCK, BLOCK)],
                        sems.at[half * DEPTH + j, p],
                    )
                )
        for copy in group:
            copy.start()
        copies.append(group)
    for p in range(pieces):
        for copy in copies[p]:
            copy.wait()
        for half in range(2):
            term = jnp.dot(x_buf[half, p], w_buf[p], preferred_element_type=jnp.float32)
            if p == 0:
                outs[half][...] = before[half][...] + term if skip else term
            else:
                outs[half][...] += term


def project(cols, x_own, x_sib, weights, token, before=(), skip=0):
    rows = x_own.shape[0]
    depth, width = weights[0].shape
    pieces = len(weights)
    out = jax.ShapeDtypeStruct((rows, width), jnp.float32)
    return pl.pallas_call(
        functools.partial(project_kernel, pieces, skip),
        in_specs=[pl.BlockSpec(memory_space=pltpu.SMEM)]
        + [pl.BlockSpec(memory_space=pl.ANY)] * (3 + pieces)
        + [pl.BlockSpec(memory_space=pltpu.VMEM)] * len(before),
        out_specs=[pl.BlockSpec(memory_space=pltpu.VMEM)] * 2,
        out_shape=[out, out],
        scratch_shapes=[
            pltpu.VMEM((2, pieces, rows, depth), jnp.bfloat16),
            pltpu.VMEM((pieces, depth, width), jnp.bfloat16),
            pltpu.SemaphoreType.DMA((2 * DEPTH + 1, pieces)),
        ],
        compiler_params=pltpu.CompilerParams(vmem_limit_bytes=56 * MIB),
        cost_estimate=SMALL,
        name="project",
    )(cols, x_own, x_sib, *weights, token, *before)


def turn_kernel(turned, scale, mine_ref, other_ref, bias_ref, cos_ref, sin_ref, order_ref, *refs):
    out_ref = refs[-1]
    rows = mine_ref.shape[0]
    both = mine_ref[...] + other_ref[...] + bias_ref[...]
    cosine, sine = cos_ref[...], sin_ref[...]
    half = HEAD_DIM // 2
    heads = []
    for head in range(both.shape[1] // HEAD_DIM):
        x = both[:, head * HEAD_DIM : (head + 1) * HEAD_DIM]
        if head < turned:
            swapped = jnp.concatenate([x[:, half:], x[:, :half]], axis=1)
            x = (x * cosine + swapped * sine) * scale
        heads.append(x.astype(out_ref.dtype))
    out_ref[:rows] = jnp.dot(
        order_ref[...], jnp.concatenate(heads, axis=1), preferred_element_type=jnp.float32
    ).astype(out_ref.dtype)
    if len(refs) > 1:
        out_ref[rows:] = refs[0][...]


def turn(turned, scale, mine, other, bias, cosine, sine, order, below=()):
    rows, width = mine.shape
    extra = sum(b.shape[0] for b in below)
    return pl.pallas_call(
        functools.partial(turn_kernel, turned, scale),
        out_shape=jax.ShapeDtypeStruct((rows + extra, width), jnp.bfloat16),
        cost_estimate=SMALL,
        name="turn",
    )(mine, other, bias, cosine, sine, order, *below)


STRIP = 128
TAKE = 128
KV_PIECES = 2 * PIECES
KEY_TILE = TAKE * KV_PIECES
SUMS = 16


UNDER = 16


def attend_kernel(top_ref, q_ref, qpos_ref, back_ref, *refs):
    pieces = refs[:KV_PIECES]
    out_ref, gathered, v_ref, k_ref, low_ref = refs[KV_PIECES:]
    size = q_ref.shape[0] * pl.num_programs(0)
    tiles = size // TAKE
    width = QPG * STRIP
    i = pl.program_id(0)

    @pl.when(i == 0)
    def _():
        under = [p[size : size + UNDER, :].astype(jnp.float32) for p in pieces]
        for t in range(tiles):
            rows = slice(t * TAKE, (t + 1) * TAKE)
            values = jnp.concatenate([p[rows, HEAD_DIM:] for p in pieces], axis=0)
            v_ref[t, :HEAD_DIM] = values.T
            v_ref[t, HEAD_DIM:] = jnp.ones((SUMS, KEY_TILE), jnp.bfloat16)
            row, lanes = t // 2, slice(t % 2 * TAKE, (t % 2 + 1) * TAKE)
            place = jnp.concatenate(
                [u[row : row + 1, lanes] * 128.0 + u[row + 2 : row + 3, lanes] for u in under],
                axis=0,
            )
            low_ref[t] = jnp.min(place).astype(jnp.int32)
            place = place.T
            for c in range(KV_PIECES):
                k_ref[t, c * TAKE : (c + 1) * TAKE] = jnp.broadcast_to(
                    place[:, c : c + 1], (TAKE, STRIP)
                )

    needed = jnp.int32(0)
    for t in range(tiles):
        needed += (low_ref[t] <= top_ref[i]).astype(jnp.int32)
    q = jnp.concatenate(
        [q_ref[:, h * HEAD_DIM : (h + 1) * HEAD_DIM] for h in range(QPG)], axis=0
    ).T
    qpos = qpos_ref[0]

    def absorb(t, state):
        best, accum = state
        rows = pl.ds(pl.multiple_of(t * TAKE, TAKE), TAKE)
        keys = jnp.concatenate([p[rows, :HEAD_DIM] for p in pieces], axis=0)
        score = jnp.dot(keys, q, preferred_element_type=jnp.float32)
        allowed = k_ref[t] <= qpos
        score = jnp.concatenate(
            [
                jnp.where(allowed, score[:, h * STRIP : (h + 1) * STRIP], -1e30)
                for h in range(QPG)
            ],
            axis=1,
        )
        newest = jnp.maximum(best, jnp.max(score, axis=0, keepdims=True))
        prob = jnp.exp2((score - newest).astype(jnp.bfloat16))
        accum = accum * jnp.exp2(best - newest) + jnp.dot(
            v_ref[t], prob, preferred_element_type=jnp.float32
        )
        return newest, accum

    state = (
        jnp.full((1, width), -1e30, jnp.float32),
        jnp.zeros((HEAD_DIM + SUMS, width), jnp.float32),
    )
    _, accum = lax.fori_loop(0, needed, absorb, state)
    result = (accum[:HEAD_DIM] / accum[HEAD_DIM : HEAD_DIM + 1]).T.astype(jnp.bfloat16)
    rows = pl.ds(pl.multiple_of(i * STRIP, STRIP), STRIP)
    for h in range(QPG):
        gathered[rows, h * HEAD_DIM : (h + 1) * HEAD_DIM] = result[h * STRIP : (h + 1) * STRIP]

    @pl.when(i == pl.num_programs(0) - 1)
    def _():
        out_ref[...] = jnp.dot(
            back_ref[...], gathered[...], preferred_element_type=jnp.float32
        ).astype(out_ref.dtype)


def attend(q, place, back, pieces):
    rows, width = q.shape
    strips, tiles = rows // STRIP, rows // TAKE
    qpos = place.reshape(strips, 1, STRIP)
    return pl.pallas_call(
        attend_kernel,
        grid_spec=pltpu.PrefetchScalarGridSpec(
            num_scalar_prefetch=1,
            grid=(strips,),
            in_specs=[
                pl.BlockSpec((STRIP, width), lambda i, *_: (i, 0)),
                pl.BlockSpec((1, 1, STRIP), lambda i, *_: (i, 0, 0)),
                pl.BlockSpec((rows, rows), lambda i, *_: (0, 0)),
            ]
            + [pl.BlockSpec((rows + UNDER, 2 * HEAD_DIM), lambda i, *_: (0, 0))] * KV_PIECES,
            out_specs=pl.BlockSpec((rows, width), lambda i, *_: (0, 0)),
            scratch_shapes=[
                pltpu.VMEM((rows, width), jnp.bfloat16),
                pltpu.VMEM((tiles, HEAD_DIM + SUMS, KEY_TILE), jnp.bfloat16),
                pltpu.VMEM((tiles, KEY_TILE, STRIP), jnp.float32),
                pltpu.SMEM((tiles,), jnp.int32),
            ],
        ),
        out_shape=jax.ShapeDtypeStruct((rows, width), jnp.bfloat16),
        compiler_params=pltpu.CompilerParams(vmem_limit_bytes=56 * MIB),
        cost_estimate=SMALL,
        name="attend",
    )(qpos[:, 0, -1], q, qpos.astype(jnp.float32), back, *pieces)


def angles(positions, width):
    half = width // 2
    freq = jnp.exp(jnp.arange(half, dtype=jnp.float32) * (-2.0 * math.log(theta_base) / width))
    phase = positions.astype(jnp.float32)[:, None] * freq[None, :]
    return (jnp.cos(phase), jnp.sin(phase))


def local(tokens, positions, stored_qkv, block_order, qkv_bias):
    rows = tokens.shape[0]
    zl, y, core = (lax.axis_index(a) for a in CTX)
    zh, x = (lax.axis_index(a) for a in HEAD)
    wide = QPG * HEAD_DIM
    half = PIECES // 2

    at = jnp.stack([zh, x]).astype(jnp.int32)
    span = stored_qkv.shape[1] // (SIZES["zh"] * SIZES["x"])
    heads = SIZES["x"]

    def give(start, width):
        cut = [
            lax.dynamic_slice_in_dim(stored_qkv, ((1 - zh) * heads + j) * span + start, width, axis=1)
            for j in range(heads)
        ]
        return jnp.concatenate(cut, axis=1)

    def along_x(parts):
        return [shift(p, "x", d) if d else p for d, p in enumerate(parts)]

    got_kv = shift(give(wide, span - wide), "zh", 1)
    got_q = shift(give(0, wide), "zh", 1)
    x_sib = shift(tokens, "core", 1)
    leaving_kv = split(at, stored_qkv, got_kv, got_kv, wide, span - wide)
    leaving_q = split(at, stored_qkv, got_q, leaving_kv[1], 0, wide)
    weight_kv = merge(at, along_x(leaving_kv), x_sib)
    weight_q = merge(at, along_x(leaving_q), weight_kv)

    rank = jnp.sum(positions[None, :] < positions[:, None], axis=1, dtype=jnp.int32)
    chosen = rank[None, :] == jnp.arange(rows, dtype=jnp.int32)[:, None]
    order = chosen.astype(jnp.bfloat16)
    back = (rank[:, None] == jnp.arange(rows, dtype=jnp.int32)[None, :]).astype(jnp.bfloat16)
    place = jnp.sum(jnp.where(chosen, positions[None, :], 0), axis=1, dtype=jnp.int32)

    place_rows = jnp.concatenate([place // 128, place % 128]).reshape(-1, 2 * HEAD_DIM)
    below = jnp.pad(place_rows, ((0, UNDER - place_rows.shape[0]), (0, 0))).astype(jnp.bfloat16)

    owners = jnp.stack([(((zl + a) % 2) * 4 + (y + b) % 4) * 2 + core for a, b in OFFSETS])
    blocks = owners[:, None] * DEPTH + jnp.arange(DEPTH, dtype=jnp.int32)[None, :]
    cols = block_order[blocks.reshape(-1)]

    cosine, sine = angles(positions, HEAD_DIM)
    cosine, sine = jnp.concatenate([cosine, cosine], axis=1), jnp.concatenate([-sine, sine], axis=1)

    scale = math.log2(math.e) / math.sqrt(HEAD_DIM)

    def start(block):
        return shift(block, "zl", 1), shift(block, "y", 1), shift(block, "y", -1)

    over, left, right = start(weight_kv)
    far = shift(weight_kv, "y", 2)
    over, far, weight_q = after([over, far, weight_q], left, right)
    near_kv = [weight_kv, over, left, right]
    late_kv = second(over, far)
    sums = project(cols, tokens, x_sib, near_kv, over)
    over, left, right = start(weight_q)
    far = shift(weight_q, "y", 2)
    own, away = project(cols, tokens, x_sib, late_kv, sums[0], sums, half)
    kv = turn(1, 1.0, own, shift(away, "core", 1), qkv_bias[None, wide:], cosine, sine, order, [below])
    over, far, kv = after([over, far, kv], left, right)
    near_q = [weight_q, over, left, right]
    late_q = second(over, far)
    over, left, right = start(kv)
    sums = project(cols, tokens, x_sib, near_q, kv)
    kv, over = after([kv, over], left, right, *late_q, sums[0])
    near = [kv, over, left, right]
    late = [shift(kv, "y", 2), shift(over, "y", 1), shift(over, "y", -1), shift(over, "y", 2)]
    own, away = project(cols, tokens, x_sib, late_q, over, sums, half)
    *pieces, away = after([*near, *late, away], own)
    pieces += [shift(b, "core", 1) for b in pieces]
    q = turn(QPG, scale, own, shift(away, "core", 1), qkv_bias[None, :wide], cosine, sine, order)
    return attend(q, place, back, pieces)


def solution(mesh):
    fine = Mesh(mesh.devices.reshape(tuple(SIZES.values())), tuple(SIZES))
    placed = (P(CTX, None), P(CTX), P(CTX + HEAD, None), P(), P(HEAD))
    return jax.shard_map(
        local, mesh=fine, in_specs=placed, out_specs=P(CTX, HEAD), check_vma=False
    )
```

time: 323 us -> 171 us (0.53)
  the two profiles are of different devices: /device:TPU:0 before, /device:TPU:7 now
where the time goes in v2:
time: 171 us
  Pallas kernels  67.2 us (39%)
  starting transfers between devices  44.9 us (26%)
  waiting for transfers between devices  37.4 us (22%)
  local copies, waits for them, and re-layouts  15 us (9%)
  other arithmetic  5.46 us (3%)
    ppermute x40, starting transfers between devices, shift(): lax.ppermute(block, axis, [(i, (i + distance) % size) for i in range(size)])  44.9 us
    ppermute x40, waiting for transfers between devices, shift(): lax.ppermute(block, axis, [(i, (i + distance) % size) for i in range(size)])  37.4 us
    pallas_call x1, Pallas kernels, attend(): pl.pallas_call(attend_kernel, grid_spec=pltpu.PrefetchScalarGridSpec(num_...  30.2 us
    pallas_call x4, Pallas kernels, project(): pl.pallas_call(functools.partial(project_kernel, pieces, skip), in_specs=...  23.6 us
    unnamed x88, local copies, waits for them, and re-layouts  9.78 us
    pallas_call x2, Pallas kernels, turn(): pl.pallas_call(functools.partial(turn_kernel, turned, scale), out_shape=j...  5.92 us
    pallas_call x2, Pallas kernels, split(): pl.pallas_call(functools.partial(split_kernel, start), in_specs=[pl.Block...  3.91 us
    pallas_call x2, Pallas kernels, merge(): pl.pallas_call(merge_kernel, in_specs=[pl.BlockSpec(memory_space=pltpu.SM...  3.6 us
  transfers between devices with their start and end apart: 40, of which 11 were waited for; matrix products, arithmetic and copies ran while one was open for 6% of the time, Pallas kernels for 22%

profile of v2, /device:TPU:7, one launch (start us, length us, event | category | flops | bytes accessed | tf_op | source)
XLA Modules:
  0.0 170.5 jit_solution(16043861122266039843)
XLA Ops:
  1.5 3.7 %collective-permute-start.1 = (bf16[64,1024]{1,0:T(8,128)(2,1)S(1)}, bf16[64,1024]{1,0:T(8,128)(2,1)S(1)}, u32[]{:S(2)}, u32[]{:S(2)}) collective-permute-start(bf16[64,1024]{1,0:T(8,128)(2,1)S(1)} %pad_maximum_fusion.3), channel_id=1, source_target_pairs={{0,4},{4,0},{1,5},{5,1},{2,6},{6,2},{3,7},{7,3},{8,12},{12,8},{9,1... | collective-permute-start | bytes 393224 | tf_op jit(solution)/shard_map/ppermute | solution.py:27
  7.2 1.8 %collective-permute-done.1.got_ref.token_ref = bf16[64,1024]{1,0:T(8,128)(2,1)S(1)} collective-permute-done((bf16[64,1024]{1,0:T(8,128)(2,1)S(1)}, bf16[64,1024]{1,0:T(8,128)(2,1)S(1)}, u32[]{:S(2)}, u32[]{:S(2)}) %collective-permute-start.1) | collective-permute-done | bytes 131104 | tf_op jit(solution)/shard_map/ppermute | solution.py:27
  9.7 1.9 %split.2 = (bf16[128,256]{1,0:T(8,128)(2,1)}, bf16[128,256]{1,0:T(8,128)(2,1)}, bf16[128,256]{1,0:T(8,128)(2,1)}, bf16[128,256]{1,0:T(8,128)(2,1)}) custom-call(s32[2]{0:T(128)} %pad_add_fusion.place_ref, bf16[64,6144]{1,0:T(8,128)(2,1)} %own_ref.3, bf16[64,1024]{1,0:T(8,128)(2,1)} %copy-done.22, bf16[64,1024]{1,0:T(8,128)(2,1)} %copy-done.22), custom_call_target="tpu_custom_call" | custom-call | flops 1 | bytes 1 | tf_op jit(solution)/shard_map/split/pallas_call | solution.py:66
  11.8 3.6 %collective-permute-done.7.got_ref = bf16[64,2048]{1,0:T(8,128)(2,1)S(1)} collective-permute-done((bf16[64,2048]{1,0:T(8,128)(2,1)S(1)}, bf16[64,2048]{1,0:T(8,128)(2,1)S(1)}, u32[]{:S(2)}, u32[]{:S(2)}) %collective-permute-start.7) | collective-permute-done | bytes 262176 | tf_op jit(solution)/shard_map/ppermute | solution.py:27
  16.0 2.0 %split.3 = (bf16[128,512]{1,0:T(8,128)(2,1)}, bf16[128,512]{1,0:T(8,128)(2,1)}, bf16[128,512]{1,0:T(8,128)(2,1)}, bf16[128,512]{1,0:T(8,128)(2,1)}) custom-call(s32[2]{0:T(128)} %pad_add_fusion.place_ref, bf16[64,6144]{1,0:T(8,128)(2,1)} %own_ref.3, bf16[64,2048]{1,0:T(8,128)(2,1)} %copy-done.34, bf16[128,256]{1,0:T(8,128)(2,1)} %get-tuple-element.39.token_ref), custom_call_target="tpu_custom_call" | custom-call | flops 1 | bytes 1 | tf_op jit(solution)/shard_map/split/pallas_call | solution.py:66
  19.5 1.9 %collective-permute-start.4 = (bf16[128,256]{1,0:T(8,128)(2,1)}, bf16[128,256]{1,0:T(8,128)(2,1)S(1)}, u32[]{:S(2)}, u32[]{:S(2)}) collective-permute-start(bf16[128,256]{1,0:T(8,128)(2,1)} %get-tuple-element.41), channel_id=1, source_target_pairs={{0,3},{1,0},{2,1},{3,2},{4,7},{5,4},{6,5},{7,6},{8,11},{9,8},{10,9... | collective-permute-start | bytes 196616 | tf_op jit(solution)/shard_map/ppermute | solution.py:27
  22.1 1.9 %collective-permute-done.3.refs_2_ = bf16[128,256]{1,0:T(8,128)(2,1)S(1)} collective-permute-done((bf16[128,256]{1,0:T(8,128)(2,1)}, bf16[128,256]{1,0:T(8,128)(2,1)S(1)}, u32[]{:S(2)}, u32[]{:S(2)}) %collective-permute-start.3) | collective-permute-done | bytes 65568 | tf_op jit(solution)/shard_map/ppermute | solution.py:27
  24.1 2.5 %collective-permute-done.4.refs_3_ = bf16[128,256]{1,0:T(8,128)(2,1)S(1)} collective-permute-done((bf16[128,256]{1,0:T(8,128)(2,1)}, bf16[128,256]{1,0:T(8,128)(2,1)S(1)}, u32[]{:S(2)}, u32[]{:S(2)}) %collective-permute-start.4) | collective-permute-done | bytes 65568 | tf_op jit(solution)/shard_map/ppermute | solution.py:27
  27.2 1.7 merge.2.refs_4_.refs_0_
  28.8 1.3 collective-permute-start.11
  30.1 1.4 collective-permute-start.12
  32.3 1.6 collective-permute-start.6
  34.5 5.1 %collective-permute-done.9.refs_2_ = bf16[128,512]{1,0:T(8,128)(2,1)S(1)} collective-permute-done((bf16[128,512]{1,0:T(8,128)(2,1)S(1)}, bf16[128,512]{1,0:T(8,128)(2,1)S(1)}, u32[]{:S(2)}, u32[]{:S(2)}) %collective-permute-start.9) | collective-permute-done | bytes 131104 | tf_op jit(solution)/shard_map/ppermute | solution.py:27
  40.3 1.9 %merge.3.refs_2_ = bf16[512,512]{1,0:T(8,128)(2,1)} custom-call(s32[2]{0:T(128)} %pad_add_fusion.place_ref, bf16[128,512]{1,0:T(8,128)(2,1)} %get-tuple-element.42.refs_0_, bf16[128,512]{1,0:T(8,128)(2,1)} %copy-done.36, bf16[128,512]{1,0:T(8,128)(2,1)} %copy-done.37, bf16[128,512]{1,0:T(8,128)(2,1)} %copy-done.35, bf16[512,256]{1,0:T(8,128)(2,1)} %merge.2.refs_4_.refs_0_), custom_call_target="tpu_custom_call" | custom-call | flops 1 | bytes 1 | tf_op jit(solution)/shard_map/merge/pallas_call | solution.py:93
  44.6 2.1 %collective-permute-start.16 = (bf16[512,256]{1,0:T(8,128)(2,1)}, bf16[512,256]{1,0:T(8,128)(2,1)S(1)}, u32[]{:S(2)}, u32[]{:S(2)}) collective-permute-start(bf16[512,256]{1,0:T(8,128)(2,1)} %get-tuple-element.48.refs_1_.refs_4_), channel_id=1, source_target_pairs={{0,48},{16,0},{32,16},{48,32},{1,49},{17,1},{33,17},{49,33},{2,50}... | collective-permute-start | bytes 786440 | tf_op jit(solution)/shard_map/ppermute | solution.py:27
  50.5 5.0 %project.4 = (f32[512,256]{1,0:T(8,128)}, f32[512,256]{1,0:T(8,128)}) custom-call(s32[32]{0:T(128)} %gather_fusion, bf16[512,8192]{1,0:T(8,128)(2,1)} %x_own.7, bf16[512,8192]{1,0:T(8,128)(2,1)} %collective-permute-done.refs_4_.x_sib, bf16[512,256]{1,0:T(8,128)(2,1)} %merge.2.refs_4_.refs_0_, bf16[512,256]{1,0:T(8,128)(2,1)} %get-tuple-element.48.refs_1_.refs_4_, ...), custom_call_target="tpu_custom_call" | custom-call | flops 1 | bytes 1 | tf_op jit(solution)/shard_map/project/pallas_call | solution.py:149
  56.2 2.1 %collective-permute-start.20 = (bf16[512,512]{1,0:T(8,128)(2,1)S(1)}, bf16[512,512]{1,0:T(8,128)(2,1)S(1)}, u32[]{:S(2)}, u32[]{:S(2)}) collective-permute-start(bf16[512,512]{1,0:T(8,128)(2,1)S(1)} %copy-done.1), channel_id=1, source_target_pairs={{0,48},{16,0},{32,16},{48,32},{1,49},{17,1},{33,17},{49,33},{2,50}... | collective-permute-start | bytes 1572872 | tf_op jit(solution)/shard_map/ppermute | solution.py:27
  59.0 5.6 %project.5 = (f32[512,256]{1,0:T(8,128)}, f32[512,256]{1,0:T(8,128)}) custom-call(s32[32]{0:T(128)} %gather_fusion, bf16[512,8192]{1,0:T(8,128)(2,1)} %x_own.7, bf16[512,8192]{1,0:T(8,128)(2,1)} %collective-permute-done.refs_4_.x_sib, bf16[512,256]{1,0:T(8,128)(2,1)} %get-tuple-element.47.refs_0_, bf16[512,256]{1,0:T(8,128)(2,1)} %copy-done.31, ...), custom_call_target="tpu_custom_call" | custom-call | flops 1 | bytes 1 | tf_op jit(solution)/shard_map/project/pallas_call | solution.py:149
  64.7 10.7 %collective-permute-start.18 = (f32[512,256]{1,0:T(8,128)}, f32[512,256]{1,0:T(8,128)S(1)}, u32[]{:S(2)}, u32[]{:S(2)}) collective-permute-start(f32[512,256]{1,0:T(8,128)} %get-tuple-element.52), channel_id=1, source_target_pairs={{0,8},{8,0},{1,9},{9,1},{2,10},{10,2},{3,11},{11,3},{4,12},{12,4},... | collective-permute-start | bytes 1572872 | tf_op jit(solution)/shard_map/ppermute | solution.py:27
  79.5 2.6 %turn.2.refs_2_ = bf16[528,256]{1,0:T(8,128)(2,1)} custom-call(f32[512,256]{1,0:T(8,128)} %get-tuple-element.51.mine_ref, f32[512,256]{1,0:T(8,128)} %copy-done.21, f32[1,256]{1,0:T(1,128)} %bitcast.18, f32[512,128]{1,0:T(8,128)} %get-tuple-element.86.cos_ref, f32[512,128]{1,0:T(8,128)} %get-tuple-element.87.sin_ref, ...), custom_call_target="tpu_custom_call" | custom-call | flops 1 | bytes 1 | tf_op jit(solution)/shard_map/turn/pallas_call | solution.py:190
  84.9 2.7 %collective-permute-start.22 = (bf16[512,512]{1,0:T(8,128)(2,1)}, bf16[512,512]{1,0:T(8,128)(2,1)S(1)}, u32[]{:S(2)}, u32[]{:S(2)}) collective-permute-start(bf16[512,512]{1,0:T(8,128)(2,1)} %get-tuple-element.54.refs_1_), channel_id=1, source_target_pairs={{0,48},{16,0},{32,16},{48,32},{1,49},{17,1},{33,17},{49,33},{2,50}... | collective-permute-start | bytes 1572872 | tf_op jit(solution)/shard_map/ppermute | solution.py:27
  88.3 4.2 %collective-permute-done.24.refs_1_ = bf16[528,256]{1,0:T(8,128)(2,1)S(1)} collective-permute-done((bf16[528,256]{1,0:T(8,128)(2,1)}, bf16[528,256]{1,0:T(8,128)(2,1)S(1)}, u32[]{:S(2)}, u32[]{:S(2)}) %collective-permute-start.24) | collective-permute-done | bytes 270368 | tf_op jit(solution)/shard_map/ppermute | solution.py:27
  92.4 6.0 %project.6 = (f32[512,512]{1,0:T(8,128)}, f32[512,512]{1,0:T(8,128)}) custom-call(s32[32]{0:T(128)} %gather_fusion, bf16[512,8192]{1,0:T(8,128)(2,1)} %x_own.7, bf16[512,8192]{1,0:T(8,128)(2,1)} %collective-permute-done.refs_4_.x_sib, bf16[512,512]{1,0:T(8,128)(2,1)} %get-tuple-element.46.refs_0_, bf16[512,512]{1,0:T(8,128)(2,1)} %get-tuple-element.54.refs_1_, ...), custom_call_target="tpu_custom_call" | custom-call | flops 1 | bytes 1 | tf_op jit(solution)/shard_map/project/pallas_call | solution.py:149
  98.5 6.8 %collective-permute-done.25.refs_2_ = bf16[528,256]{1,0:T(8,128)(2,1)S(1)} collective-permute-done((bf16[528,256]{1,0:T(8,128)(2,1)}, bf16[528,256]{1,0:T(8,128)(2,1)S(1)}, u32[]{:S(2)}, u32[]{:S(2)}) %collective-permute-start.25) | collective-permute-done | bytes 270368 | tf_op jit(solution)/shard_map/ppermute | solution.py:27
  107.8 1.7 %collective-permute-start.28 = (bf16[528,256]{1,0:T(8,128)(2,1)}, bf16[528,256]{1,0:T(8,128)(2,1)S(1)}, u32[]{:S(2)}, u32[]{:S(2)}) collective-permute-start(bf16[528,256]{1,0:T(8,128)(2,1)} %get-tuple-element.57.refs_4_.refs_1_), channel_id=1, source_target_pairs={{0,16},{16,32},{32,48},{48,0},{1,17},{17,33},{33,49},{49,1},{2,18}... | collective-permute-start | bytes 811016 | tf_op jit(solution)/shard_map/ppermute | solution.py:27
  111.3 6.9 %project.7 = (f32[512,512]{1,0:T(8,128)}, f32[512,512]{1,0:T(8,128)}) custom-call(s32[32]{0:T(128)} %gather_fusion, bf16[512,8192]{1,0:T(8,128)(2,1)} %x_own.7, bf16[512,8192]{1,0:T(8,128)(2,1)} %collective-permute-done.refs_4_.x_sib, bf16[512,512]{1,0:T(8,128)(2,1)} %get-tuple-element.53.refs_4_.refs_0_, bf16[512,512]{1,0:T(8,128)(2,1)} %copy-done.10, ...), custom_call_target="tpu_custom_call" | custom-call | flops 1 | bytes 1 | tf_op jit(solution)/shard_map/project/pallas_call | solution.py:149
  118.2 5.8 %collective-permute-done.28.refs_5_ = bf16[528,256]{1,0:T(8,128)(2,1)S(1)} collective-permute-done((bf16[528,256]{1,0:T(8,128)(2,1)}, bf16[528,256]{1,0:T(8,128)(2,1)S(1)}, u32[]{:S(2)}, u32[]{:S(2)}) %collective-permute-start.28) | collective-permute-done | bytes 270368 | tf_op jit(solution)/shard_map/ppermute | solution.py:27
  124.1 2.8 %collective-permute-done.30.refs_7_ = bf16[528,256]{1,0:T(8,128)(2,1)S(1)} collective-permute-done((bf16[528,256]{1,0:T(8,128)(2,1)}, bf16[528,256]{1,0:T(8,128)(2,1)S(1)}, u32[]{:S(2)}, u32[]{:S(2)}) %collective-permute-start.30) | collective-permute-done | bytes 270368 | tf_op jit(solution)/shard_map/ppermute | solution.py:27
  127.5 2.1 %collective-permute-start.31 = (f32[512,512]{1,0:T(8,128)}, f32[512,512]{1,0:T(8,128)S(1)}, u32[]{:S(2)}, u32[]{:S(2)}) collective-permute-start(f32[512,512]{1,0:T(8,128)} %get-tuple-element.62), channel_id=1, source_target_pairs={{0,8},{8,0},{1,9},{9,1},{2,10},{10,2},{3,11},{11,3},{4,12},{12,4},... | collective-permute-start | bytes 3145736 | tf_op jit(solution)/shard_map/ppermute | solution.py:27
  130.6 1.9 %collective-permute-done.32.refs_8_ = bf16[528,256]{1,0:T(8,128)(2,1)S(1)} collective-permute-done((bf16[528,256]{1,0:T(8,128)(2,1)}, bf16[528,256]{1,0:T(8,128)(2,1)S(1)}, u32[]{:S(2)}, u32[]{:S(2)}) %collective-permute-start.32) | collective-permute-done | bytes 270368 | tf_op jit(solution)/shard_map/ppermute | solution.py:27
  135.9 3.3 %turn.3.q_ref = bf16[512,512]{1,0:T(8,128)(2,1)} custom-call(f32[512,512]{1,0:T(8,128)} %get-tuple-element.59.refs_9_.mine_ref, f32[512,512]{1,0:T(8,128)} %copy-done.18, f32[1,512]{1,0:T(1,128)} %bitcast.17, f32[512,128]{1,0:T(8,128)} %get-tuple-element.86.cos_ref, f32[512,128]{1,0:T(8,128)} %get-tuple-element.87.sin_ref, ...), custom_call_target="tpu_custom_call" | custom-call | flops 1 | bytes 1 | tf_op jit(solution)/shard_map/turn/pallas_call | solution.py:190
  140.3 30.2 %attend.1 = bf16[512,512]{1,0:T(8,128)(2,1)} custom-call(s32[4]{0:T(128)} %slice_reduce_fusion.top_ref, bf16[512,512]{1,0:T(8,128)(2,1)} %turn.3.q_ref, f32[4,1,128]{2,1,0:T(1,128)} %convert_element_type.19.qpos_ref, bf16[512,512]{1,0:T(8,128)(2,1)} %get-tuple-element.82.back_ref, bf16[528,256]{1,0:T(8,128)(2,1)} %get-tuple-element.63.refs_0_, ...), custom_call_target="tpu_custom_call" | custom-call | flops 1 | bytes 1 | tf_op jit(solution)/shard_map/attend/pallas_call | solution.py:285
  (177 shorter events, 35.1 us)
Async XLA Ops:
  0.0 26.6 %collective-permute-start = (bf16[512,8192]{1,0:T(8,128)(2,1)}, bf16[512,8192]{1,0:T(8,128)(2,1)}, u32[]{:S(2)}, u32[]{:S(2)}) collective-permute-start(bf16[512,8192]{1,0:T(8,128)(2,1)} %x_own.7), channel_id=1, source_target_pairs={{0,8},{8,0},{1,9},{9,1},{2,10},{10,2},{3,11},{11,3},{4,12},{12,4},... | collective-permute-start | bytes 25165832 | tf_op jit(solution)/shard_map/ppermute | solution.py:27
  1.5 7.5 %collective-permute-start.1 = (bf16[64,1024]{1,0:T(8,128)(2,1)S(1)}, bf16[64,1024]{1,0:T(8,128)(2,1)S(1)}, u32[]{:S(2)}, u32[]{:S(2)}) collective-permute-start(bf16[64,1024]{1,0:T(8,128)(2,1)S(1)} %pad_maximum_fusion.3), channel_id=1, source_target_pairs={{0,4},{4,0},{1,5},{5,1},{2,6},{6,2},{3,7},{7,3},{8,12},{12,8},{9,1... | collective-permute-start | bytes 393224 | tf_op jit(solution)/shard_map/ppermute | solution.py:27
  6.2 9.2 %collective-permute-start.7 = (bf16[64,2048]{1,0:T(8,128)(2,1)S(1)}, bf16[64,2048]{1,0:T(8,128)(2,1)S(1)}, u32[]{:S(2)}, u32[]{:S(2)}) collective-permute-start(bf16[64,2048]{1,0:T(8,128)(2,1)S(1)} %pad_maximum_fusion), channel_id=1, source_target_pairs={{0,4},{4,0},{1,5},{5,1},{2,6},{6,2},{3,7},{7,3},{8,12},{12,8},{9,1... | collective-permute-start | bytes 786440 | tf_op jit(solution)/shard_map/ppermute | solution.py:27
  11.6 9.8 %collective-permute-start.2 = (bf16[128,256]{1,0:T(8,128)(2,1)}, bf16[128,256]{1,0:T(8,128)(2,1)S(1)}, u32[]{:S(2)}, u32[]{:S(2)}) collective-permute-start(bf16[128,256]{1,0:T(8,128)(2,1)} %get-tuple-element.39.token_ref), channel_id=1, source_target_pairs={{0,1},{1,2},{2,3},{3,0},{4,5},{5,6},{6,7},{7,4},{8,9},{9,10},{10,1... | collective-permute-start | bytes 196616 | tf_op jit(solution)/shard_map/ppermute | solution.py:27
  18.1 14.3 %collective-permute-start.10 = (bf16[128,512]{1,0:T(8,128)(2,1)}, bf16[128,512]{1,0:T(8,128)(2,1)S(1)}, u32[]{:S(2)}, u32[]{:S(2)}) collective-permute-start(bf16[128,512]{1,0:T(8,128)(2,1)} %get-tuple-element.45), channel_id=1, source_target_pairs={{0,3},{1,0},{2,1},{3,2},{4,7},{5,4},{6,5},{7,6},{8,11},{9,8},{10,9... | collective-permute-start | bytes 393224 | tf_op jit(solution)/shard_map/ppermute | solution.py:27
  19.5 7.1 %collective-permute-start.4 = (bf16[128,256]{1,0:T(8,128)(2,1)}, bf16[128,256]{1,0:T(8,128)(2,1)S(1)}, u32[]{:S(2)}, u32[]{:S(2)}) collective-permute-start(bf16[128,256]{1,0:T(8,128)(2,1)} %get-tuple-element.41), channel_id=1, source_target_pairs={{0,3},{1,0},{2,1},{3,2},{4,7},{5,4},{6,5},{7,6},{8,11},{9,8},{10,9... | collective-permute-start | bytes 196616 | tf_op jit(solution)/shard_map/ppermute | solution.py:27
  21.3 12.9 %collective-permute-start.8 = (bf16[128,512]{1,0:T(8,128)(2,1)}, bf16[128,512]{1,0:T(8,128)(2,1)S(1)}, u32[]{:S(2)}, u32[]{:S(2)}) collective-permute-start(bf16[128,512]{1,0:T(8,128)(2,1)} %get-tuple-element.43), channel_id=1, source_target_pairs={{0,1},{1,2},{2,3},{3,0},{4,5},{5,6},{6,7},{7,4},{8,9},{9,10},{10,1... | collective-permute-start | bytes 393224 | tf_op jit(solution)/shard_map/ppermute | solution.py:27
  28.8 13.4 %collective-permute-start.11 = (bf16[512,256]{1,0:T(8,128)(2,1)}, bf16[512,256]{1,0:T(8,128)(2,1)S(1)}, u32[]{:S(2)}, u32[]{:S(2)}) collective-permute-start(bf16[512,256]{1,0:T(8,128)(2,1)} %merge.2.refs_4_.refs_0_), channel_id=1, source_target_pairs={{0,16},{16,32},{32,48},{48,0},{1,17},{17,33},{33,49},{49,1},{2,18}... | collective-permute-start | bytes 786440 | tf_op jit(solution)/shard_map/ppermute | solution.py:27
  30.1 12.1 %collective-permute-start.12 = (bf16[512,256]{1,0:T(8,128)(2,1)}, bf16[512,256]{1,0:T(8,128)(2,1)S(1)}, u32[]{:S(2)}, u32[]{:S(2)}) collective-permute-start(bf16[512,256]{1,0:T(8,128)(2,1)} %merge.2.refs_4_.refs_0_), channel_id=1, source_target_pairs={{0,48},{16,0},{32,16},{48,32},{1,49},{17,1},{33,17},{49,33},{2,50}... | collective-permute-start | bytes 786440 | tf_op jit(solution)/shard_map/ppermute | solution.py:27
  31.6 10.7 %collective-permute-start.5 = (bf16[512,256]{1,0:T(8,128)(2,1)}, bf16[512,256]{1,0:T(8,128)(2,1)S(1)}, u32[]{:S(2)}, u32[]{:S(2)}) collective-permute-start(bf16[512,256]{1,0:T(8,128)(2,1)} %merge.2.refs_4_.refs_0_), channel_id=1, source_target_pairs={{0,64},{64,0},{1,65},{65,1},{2,66},{66,2},{3,67},{67,3},{4,68},{68... | collective-permute-start | bytes 786440 | tf_op jit(solution)/shard_map/ppermute | solution.py:27
  32.3 10.9 %collective-permute-start.6 = (bf16[512,256]{1,0:T(8,128)(2,1)}, bf16[512,256]{1,0:T(8,128)(2,1)S(1)}, u32[]{:S(2)}, u32[]{:S(2)}) collective-permute-start(bf16[512,256]{1,0:T(8,128)(2,1)} %merge.2.refs_4_.refs_0_), channel_id=1, source_target_pairs={{0,32},{16,48},{32,0},{48,16},{1,33},{17,49},{33,1},{49,17},{2,34}... | collective-permute-start | bytes 786440 | tf_op jit(solution)/shard_map/ppermute | solution.py:27
  44.0 11.6 %collective-permute-start.15 = (bf16[512,256]{1,0:T(8,128)(2,1)}, bf16[512,256]{1,0:T(8,128)(2,1)S(1)}, u32[]{:S(2)}, u32[]{:S(2)}) collective-permute-start(bf16[512,256]{1,0:T(8,128)(2,1)} %get-tuple-element.48.refs_1_.refs_4_), channel_id=1, source_target_pairs={{0,16},{16,32},{32,48},{48,0},{1,17},{17,33},{33,49},{49,1},{2,18}... | collective-permute-start | bytes 786440 | tf_op jit(solution)/shard_map/ppermute | solution.py:27
  44.6 11.7 %collective-permute-start.16 = (bf16[512,256]{1,0:T(8,128)(2,1)}, bf16[512,256]{1,0:T(8,128)(2,1)S(1)}, u32[]{:S(2)}, u32[]{:S(2)}) collective-permute-start(bf16[512,256]{1,0:T(8,128)(2,1)} %get-tuple-element.48.refs_1_.refs_4_), channel_id=1, source_target_pairs={{0,48},{16,0},{32,16},{48,32},{1,49},{17,1},{33,17},{49,33},{2,50}... | collective-permute-start | bytes 786440 | tf_op jit(solution)/shard_map/ppermute | solution.py:27
  46.7 11.7 %collective-permute-start.17 = (bf16[512,256]{1,0:T(8,128)(2,1)}, bf16[512,256]{1,0:T(8,128)(2,1)S(1)}, u32[]{:S(2)}, u32[]{:S(2)}) collective-permute-start(bf16[512,256]{1,0:T(8,128)(2,1)} %get-tuple-element.47.refs_0_), channel_id=1, source_target_pairs={{0,64},{64,0},{1,65},{65,1},{2,66},{66,2},{3,67},{67,3},{4,68},{68... | collective-permute-start | bytes 786440 | tf_op jit(solution)/shard_map/ppermute | solution.py:27
  49.7 32.4 %collective-permute-start.13 = (bf16[512,512]{1,0:T(8,128)(2,1)}, bf16[512,512]{1,0:T(8,128)(2,1)S(1)}, u32[]{:S(2)}, u32[]{:S(2)}) collective-permute-start(bf16[512,512]{1,0:T(8,128)(2,1)} %get-tuple-element.46.refs_0_), channel_id=1, source_target_pairs={{0,64},{64,0},{1,65},{65,1},{2,66},{66,2},{3,67},{67,3},{4,68},{68... | collective-permute-start | bytes 1572872 | tf_op jit(solution)/shard_map/ppermute | solution.py:27
  50.5 31.6 %collective-permute-start.14 = (bf16[512,512]{1,0:T(8,128)(2,1)}, bf16[512,512]{1,0:T(8,128)(2,1)S(1)}, u32[]{:S(2)}, u32[]{:S(2)}) collective-permute-start(bf16[512,512]{1,0:T(8,128)(2,1)} %get-tuple-element.46.refs_0_), channel_id=1, source_target_pairs={{0,32},{16,48},{32,0},{48,16},{1,33},{17,49},{33,1},{49,17},{2,34}... | collective-permute-start | bytes 1572872 | tf_op jit(solution)/shard_map/ppermute | solution.py:27
  55.6 26.6 %collective-permute-start.19 = (bf16[512,512]{1,0:T(8,128)(2,1)S(1)}, bf16[512,512]{1,0:T(8,128)(2,1)S(1)}, u32[]{:S(2)}, u32[]{:S(2)}) collective-permute-start(bf16[512,512]{1,0:T(8,128)(2,1)S(1)} %copy-done.1), channel_id=1, source_target_pairs={{0,16},{16,32},{32,48},{48,0},{1,17},{17,33},{33,49},{49,1},{2,18}... | collective-permute-start | bytes 1572872 | tf_op jit(solution)/shard_map/ppermute | solution.py:27
  56.2 26.0 %collective-permute-start.20 = (bf16[512,512]{1,0:T(8,128)(2,1)S(1)}, bf16[512,512]{1,0:T(8,128)(2,1)S(1)}, u32[]{:S(2)}, u32[]{:S(2)}) collective-permute-start(bf16[512,512]{1,0:T(8,128)(2,1)S(1)} %copy-done.1), channel_id=1, source_target_pairs={{0,48},{16,0},{32,16},{48,32},{1,49},{17,1},{33,17},{49,33},{2,50}... | collective-permute-start | bytes 1572872 | tf_op jit(solution)/shard_map/ppermute | solution.py:27
  64.7 14.1 %collective-permute-start.18 = (f32[512,256]{1,0:T(8,128)}, f32[512,256]{1,0:T(8,128)S(1)}, u32[]{:S(2)}, u32[]{:S(2)}) collective-permute-start(f32[512,256]{1,0:T(8,128)} %get-tuple-element.52), channel_id=1, source_target_pairs={{0,8},{8,0},{1,9},{9,1},{2,10},{10,2},{3,11},{11,3},{4,12},{12,4},... | collective-permute-start | bytes 1572872 | tf_op jit(solution)/shard_map/ppermute | solution.py:27
  84.1 8.3 %collective-permute-start.24 = (bf16[528,256]{1,0:T(8,128)(2,1)}, bf16[528,256]{1,0:T(8,128)(2,1)S(1)}, u32[]{:S(2)}, u32[]{:S(2)}) collective-permute-start(bf16[528,256]{1,0:T(8,128)(2,1)} %get-tuple-element.55.refs_4_.refs_0_), channel_id=1, source_target_pairs={{0,64},{64,0},{1,65},{65,1},{2,66},{66,2},{3,67},{67,3},{4,68},{68... | collective-permute-start | bytes 811016 | tf_op jit(solution)/shard_map/ppermute | solution.py:27
  84.9 20.4 %collective-permute-start.21 = (bf16[512,512]{1,0:T(8,128)(2,1)}, bf16[512,512]{1,0:T(8,128)(2,1)S(1)}, u32[]{:S(2)}, u32[]{:S(2)}) collective-permute-start(bf16[512,512]{1,0:T(8,128)(2,1)} %get-tuple-element.54.refs_1_), channel_id=1, source_target_pairs={{0,16},{16,32},{32,48},{48,0},{1,17},{17,33},{33,49},{49,1},{2,18}... | collective-permute-start | bytes 1572872 | tf_op jit(solution)/shard_map/ppermute | solution.py:27
  84.9 20.4 %collective-permute-start.22 = (bf16[512,512]{1,0:T(8,128)(2,1)}, bf16[512,512]{1,0:T(8,128)(2,1)S(1)}, u32[]{:S(2)}, u32[]{:S(2)}) collective-permute-start(bf16[512,512]{1,0:T(8,128)(2,1)} %get-tuple-element.54.refs_1_), channel_id=1, source_target_pairs={{0,48},{16,0},{32,16},{48,32},{1,49},{17,1},{33,17},{49,33},{2,50}... | collective-permute-start | bytes 1572872 | tf_op jit(solution)/shard_map/ppermute | solution.py:27
  87.6 17.8 %collective-permute-start.23 = (bf16[512,512]{1,0:T(8,128)(2,1)}, bf16[512,512]{1,0:T(8,128)(2,1)S(1)}, u32[]{:S(2)}, u32[]{:S(2)}) collective-permute-start(bf16[512,512]{1,0:T(8,128)(2,1)} %get-tuple-element.53.refs_4_.refs_0_), channel_id=1, source_target_pairs={{0,64},{64,0},{1,65},{65,1},{2,66},{66,2},{3,67},{67,3},{4,68},{68... | collective-permute-start | bytes 1572872 | tf_op jit(solution)/shard_map/ppermute | solution.py:27
  88.3 17.0 %collective-permute-start.25 = (bf16[528,256]{1,0:T(8,128)(2,1)}, bf16[528,256]{1,0:T(8,128)(2,1)S(1)}, u32[]{:S(2)}, u32[]{:S(2)}) collective-permute-start(bf16[528,256]{1,0:T(8,128)(2,1)} %get-tuple-element.55.refs_4_.refs_0_), channel_id=1, source_target_pairs={{0,16},{16,32},{32,48},{48,0},{1,17},{17,33},{33,49},{49,1},{2,18}... | collective-permute-start | bytes 811016 | tf_op jit(solution)/shard_map/ppermute | solution.py:27
  92.4 12.9 %collective-permute-start.26 = (bf16[528,256]{1,0:T(8,128)(2,1)}, bf16[528,256]{1,0:T(8,128)(2,1)S(1)}, u32[]{:S(2)}, u32[]{:S(2)}) collective-permute-start(bf16[528,256]{1,0:T(8,128)(2,1)} %get-tuple-element.55.refs_4_.refs_0_), channel_id=1, source_target_pairs={{0,48},{16,0},{32,16},{48,32},{1,49},{17,1},{33,17},{49,33},{2,50}... | collective-permute-start | bytes 811016 | tf_op jit(solution)/shard_map/ppermute | solution.py:27
  106.6 11.6 %collective-permute-start.27 = (bf16[528,256]{1,0:T(8,128)(2,1)}, bf16[528,256]{1,0:T(8,128)(2,1)S(1)}, u32[]{:S(2)}, u32[]{:S(2)}) collective-permute-start(bf16[528,256]{1,0:T(8,128)(2,1)} %get-tuple-element.60.refs_0_), channel_id=1, source_target_pairs={{0,32},{16,48},{32,0},{48,16},{1,33},{17,49},{33,1},{49,17},{2,34}... | collective-permute-start | bytes 811016 | tf_op jit(solution)/shard_map/ppermute | solution.py:27
  107.8 16.3 %collective-permute-start.28 = (bf16[528,256]{1,0:T(8,128)(2,1)}, bf16[528,256]{1,0:T(8,128)(2,1)S(1)}, u32[]{:S(2)}, u32[]{:S(2)}) collective-permute-start(bf16[528,256]{1,0:T(8,128)(2,1)} %get-tuple-element.57.refs_4_.refs_1_), channel_id=1, source_target_pairs={{0,16},{16,32},{32,48},{48,0},{1,17},{17,33},{33,49},{49,1},{2,18}... | collective-permute-start | bytes 811016 | tf_op jit(solution)/shard_map/ppermute | solution.py:27
  109.5 14.6 %collective-permute-start.29 = (bf16[528,256]{1,0:T(8,128)(2,1)}, bf16[528,256]{1,0:T(8,128)(2,1)S(1)}, u32[]{:S(2)}, u32[]{:S(2)}) collective-permute-start(bf16[528,256]{1,0:T(8,128)(2,1)} %get-tuple-element.57.refs_4_.refs_1_), channel_id=1, source_target_pairs={{0,48},{16,0},{32,16},{48,32},{1,49},{17,1},{33,17},{49,33},{2,50}... | collective-permute-start | bytes 811016 | tf_op jit(solution)/shard_map/ppermute | solution.py:27
  110.4 16.4 %collective-permute-start.30 = (bf16[528,256]{1,0:T(8,128)(2,1)}, bf16[528,256]{1,0:T(8,128)(2,1)S(1)}, u32[]{:S(2)}, u32[]{:S(2)}) collective-permute-start(bf16[528,256]{1,0:T(8,128)(2,1)} %get-tuple-element.57.refs_4_.refs_1_), channel_id=1, source_target_pairs={{0,32},{16,48},{32,0},{48,16},{1,33},{17,49},{33,1},{49,17},{2,34}... | collective-permute-start | bytes 811016 | tf_op jit(solution)/shard_map/ppermute | solution.py:27
  130.1 9.1 %collective-permute-start.35 = (bf16[528,256]{1,0:T(8,128)(2,1)}, bf16[528,256]{1,0:T(8,128)(2,1)S(1)}, u32[]{:S(2)}, u32[]{:S(2)}) collective-permute-start(bf16[528,256]{1,0:T(8,128)(2,1)} %get-tuple-element.66.refs_3_), channel_id=1, source_target_pairs={{0,8},{8,0},{1,9},{9,1},{2,10},{10,2},{3,11},{11,3},{4,12},{12,4},... | collective-permute-start | bytes 811016 | tf_op jit(solution)/shard_map/ppermute | solution.py:27
  132.5 6.7 %collective-permute-start.36 = (bf16[528,256]{1,0:T(8,128)(2,1)}, bf16[528,256]{1,0:T(8,128)(2,1)S(1)}, u32[]{:S(2)}, u32[]{:S(2)}) collective-permute-start(bf16[528,256]{1,0:T(8,128)(2,1)} %get-tuple-element.67.refs_4_), channel_id=1, source_target_pairs={{0,8},{8,0},{1,9},{9,1},{2,10},{10,2},{3,11},{11,3},{4,12},{12,4},... | collective-permute-start | bytes 811016 | tf_op jit(solution)/shard_map/ppermute | solution.py:27
  132.9 6.3 %collective-permute-start.37 = (bf16[528,256]{1,0:T(8,128)(2,1)}, bf16[528,256]{1,0:T(8,128)(2,1)S(1)}, u32[]{:S(2)}, u32[]{:S(2)}) collective-permute-start(bf16[528,256]{1,0:T(8,128)(2,1)} %get-tuple-element.68.refs_5_), channel_id=1, source_target_pairs={{0,8},{8,0},{1,9},{9,1},{2,10},{10,2},{3,11},{11,3},{4,12},{12,4},... | collective-permute-start | bytes 811016 | tf_op jit(solution)/shard_map/ppermute | solution.py:27
  (52 other events, 246.2 us)
